TPU v7x, 128 devices: a whole 4x4x4 slice. The times are simulated.
128 devices in a mesh: lat: 8 (over x_hi, z), lon: 16 (over y, x_lo, core).
Axes of the slice: x: 4 (x_hi: 2, x_lo: 2; x = x_hi * 2 + x_lo), y: 4, z: 4, core: 2. Of those that a mesh axis runs over, the one named last changes fastest.
Arguments:
- tokens: bfloat16 [2, 128, 384, 1024], P(None, 'lat', 'lon'), may hold values from -6 to 6
- qkv_weight: bfloat16 [1024, 3072], replicated, may hold values from -0.1875 to 0.1875
- out_weight: bfloat16 [1024, 1024], replicated, may hold values from -0.1875 to 0.1875
- merge_weight: bfloat16 [4096, 1024], replicated, may hold values from -0.09375 to 0.09375
- merged_grad: bfloat16 [2, 64, 192, 1024], P(None, 'lat', 'lon'), may hold values from -6 to 6
Outputs:
- merged: bfloat16 [2, 64, 192, 1024], P(None, 'lat', 'lon')
- tokens_grad: bfloat16 [2, 128, 384, 1024], P(None, 'lat', 'lon')
- qkv_weight_grad: float32 [1024, 3072], P(('lat', 'lon'))
- out_weight_grad: float32 [1024, 1024], P(('lat', 'lon'))
All inputs are finite; a program needn't handle non-finite values.
Results may differ from a plain program's by a relative error of at most 0.02.
Values may be sent and summed in bfloat16 or wider, within the bound.
A program may use at most 192 MiB of HBM per device.

v0:
```python
import jax
import jax.numpy as jnp
from jax import lax
from jax.sharding import PartitionSpec as P

HEADS = 32
WIN = 8
SHIFT = 4


epsilon = 1e-05


def shifted(block, axis, distance):
    devices = range(lax.axis_size(axis))
    route = [((i - distance) % len(devices), i) for i in devices]
    return lax.ppermute(block, axis, route)


def normalize(grid_field):
    values = grid_field.astype(jnp.float32)
    center = jnp.mean(values, axis=-1, keepdims=True)
    spread = jnp.mean(jnp.square(values - center), axis=-1, keepdims=True)
    return ((values - center) * lax.rsqrt(spread + epsilon)).astype(jnp.bfloat16)


def window_attention(window_values, region_marks):
    windows = window_values.shape[0]
    places = window_values.shape[1]
    channels = window_values.shape[2] // 3
    head_dim = channels // HEADS
    pieces = window_values.reshape(windows, places, 3, HEADS, head_dim)
    queries = pieces[:, :, 0]
    keys_part = pieces[:, :, 1]
    values_part = pieces[:, :, 2]
    scores = jnp.einsum(
        "bqhd,bkhd->bhqk", queries, keys_part, preferred_element_type=jnp.float32
    ) * head_dim ** (-0.5)
    same_region = region_marks[:, None, :, None] == region_marks[:, None, None, :]
    weights = jnp.where(same_region, jnp.exp(scores), 0.0)
    attention = (weights / jnp.sum(weights, axis=-1, keepdims=True)).astype(jnp.bfloat16)
    mixture = jnp.einsum(
        "bhqk,bkhd->bqhd", attention, values_part, preferred_element_type=jnp.float32
    )
    return mixture.astype(jnp.bfloat16).reshape(windows, places, channels)


def to_windows(grid_field):
    lev_count, lat_rows, lon_cols, channels = grid_field.shape
    blocks = grid_field.reshape(lev_count, lat_rows // WIN, WIN, lon_cols // WIN, WIN, channels)
    blocks = blocks.transpose(1, 3, 0, 2, 4, 5)
    return blocks.reshape(lat_rows // WIN * (lon_cols // WIN), lev_count * WIN * WIN, channels)


def from_windows(blocks, lev_count, lat_rows, lon_cols):
    channels = blocks.shape[-1]
    grid_field = blocks.reshape(lat_rows // WIN, lon_cols // WIN, lev_count, WIN, WIN, channels)
    return grid_field.transpose(2, 0, 3, 1, 4, 5).reshape(lev_count, lat_rows, lon_cols, channels)


def attend_local(projected, region):
    lev_count, lat_rows, lon_cols, channels = projected.shape
    blocks = to_windows(projected)
    region_blocks = to_windows(region[..., None])[..., 0]
    mixture = window_attention(blocks, region_blocks)
    return from_windows(mixture, lev_count, lat_rows, lon_cols)


def merge(grid_field, merge_weight):
    lev_count, lat_rows, lon_cols, channels = grid_field.shape
    groups = grid_field.reshape(lev_count, lat_rows // 2, 2, lon_cols // 2, 2, channels)
    groups = groups.transpose(0, 1, 3, 4, 2, 5).reshape(
        lev_count, lat_rows // 2, lon_cols // 2, 4 * channels
    )
    normed = normalize(groups)
    result = jnp.dot(
        normed.reshape(-1, 4 * channels), merge_weight, preferred_element_type=jnp.float32
    )
    return result.astype(jnp.bfloat16).reshape(
        lev_count, lat_rows // 2, lon_cols // 2, merge_weight.shape[1]
    )


def move_strips(grid_field, strip_width, offset):
    if offset == 1:
        outgoing = grid_field[:, :, -strip_width:]
    else:
        outgoing = grid_field[:, :, :strip_width]
    arrived = shifted(outgoing, "lon", offset)
    if offset == 1:
        middle = jnp.concatenate([arrived, grid_field[:, :, :-strip_width]], axis=2)
        outgoing_rows = middle[:, -strip_width:]
    else:
        middle = jnp.concatenate([grid_field[:, :, strip_width:], arrived], axis=2)
        outgoing_rows = middle[:, :strip_width]
    arrived_rows = shifted(outgoing_rows, "lat", offset)
    if offset == 1:
        return jnp.concatenate([arrived_rows, middle[:, :-strip_width]], axis=1)
    return jnp.concatenate([middle[:, strip_width:], arrived_rows], axis=1)


def shards(tokens, qkv_weight, out_weight, merge_weight, merged_grad):
    lev_count, lat_rows, lon_cols, channels = tokens.shape
    framed = move_strips(tokens, SHIFT, 1)
    normed, norm_back = jax.vjp(normalize, framed)
    flat_norm = normed.reshape(-1, channels)
    projected = jnp.dot(flat_norm, qkv_weight, preferred_element_type=jnp.float32).astype(
        jnp.bfloat16
    )
    projected = projected.reshape(lev_count, lat_rows, lon_cols, 3 * channels)
    edge_rows = (lax.axis_index("lat") == 0) & (jnp.arange(lat_rows) < SHIFT)
    region = jnp.broadcast_to(
        edge_rows.astype(jnp.int32)[None, :, None], (lev_count, lat_rows, lon_cols)
    )
    mixture, attend_back = jax.vjp(lambda grid_values: attend_local(grid_values, region), projected)
    mixture_flat = mixture.reshape(-1, channels)
    branch = jnp.dot(mixture_flat, out_weight, preferred_element_type=jnp.float32)
    shifted_out = (framed.reshape(-1, channels).astype(jnp.float32) + branch).astype(jnp.bfloat16)
    shifted_out = shifted_out.reshape(framed.shape)
    block_out = move_strips(shifted_out, SHIFT, -1)
    merged, merge_back = jax.vjp(lambda grid_values: merge(grid_values, merge_weight), block_out)
    block_grad = merge_back(merged_grad)[0]
    framed_grad_out = move_strips(block_grad, SHIFT, 1)
    grad_rolled = framed_grad_out.reshape(-1, channels)
    mixture_grad = lax.dot_general(
        grad_rolled, out_weight, (((1,), (1,)), ((), ())), preferred_element_type=jnp.float32
    ).astype(jnp.bfloat16)
    out_terms = lax.dot_general(
        mixture_flat, grad_rolled, (((0,), (0,)), ((), ())), preferred_element_type=jnp.float32
    )
    projected_grad = attend_back(mixture_grad.reshape(mixture.shape))[0].reshape(-1, 3 * channels)
    qkv_terms = lax.dot_general(
        flat_norm, projected_grad, (((0,), (0,)), ((), ())), preferred_element_type=jnp.float32
    )
    normed_grad = lax.dot_general(
        projected_grad, qkv_weight, (((1,), (1,)), ((), ())), preferred_element_type=jnp.float32
    ).astype(jnp.bfloat16)
    input_part = norm_back(normed_grad.reshape(normed.shape))[0].reshape(-1, channels)
    framed_grad = (grad_rolled.astype(jnp.float32) + input_part.astype(jnp.float32)).astype(
        jnp.bfloat16
    )
    tokens_grad = move_strips(framed_grad.reshape(framed.shape), SHIFT, -1)
    qkv_weight_grad, out_weight_grad = (
        lax.psum_scatter(qkv_terms, ("lat", "lon"), scatter_dimension=0, tiled=True),
        lax.psum_scatter(out_terms, ("lat", "lon"), scatter_dimension=0, tiled=True),
    )
    return (merged, tokens_grad, qkv_weight_grad, out_weight_grad)


def solution(mesh):
    in_specs = (P(None, "lat", "lon", None), P(), P(), P(), P(None, "lat", "lon", None))
    out_specs = (
        P(None, "lat", "lon", None),
        P(None, "lat", "lon", None),
        P(("lat", "lon"), None),
        P(("lat", "lon"), None),
    )
    return jax.shard_map(shards, mesh=mesh, in_specs=in_specs, out_specs=out_specs, check_vma=False)
```

profile of v0, /device:TPU:1, one launch (start us, length us, event | category | flops | bytes accessed | tf_op | source)
XLA Modules:
  0.0 1540.2 jit_solution(4392012440410617178)
XLA Ops:
  17.7 9.6 collective-permute-done.1
  34.3 8.2 convolution_convert_fusion
  45.2 21.3 %reshape.250 = bf16[6,128,3,32,32]{4,3,2,1,0:T(8,128)(2,1)} reshape(bf16[2,3,2,8,8,3072]{5,4,3,2,1,0:T(8,128)(2,1)} %bitcast.127) | data formatting | bytes 9437184 | tf_op jit(solution)/shard_map/jvp()/reshape;jvp()/reshape | solution.py:32
  66.5 14.3 fusion.56
  80.8 8.6 copy.41
  89.4 8.6 copy.42
  98.0 8.6 copy.40
  106.6 5.0 fusion.7
  122.0 9.9 copy.22
  131.9 9.6 reshape.251
  147.2 4.4 collective-permute-start.2
  159.6 8.0 fusion.8
  167.6 6.1 reshape.264
  177.1 5.2 reshape.266
  182.3 4.5 fusion.54
  186.8 5.6 multiply_reduce_fusion.1
  198.1 7.2 fusion.36
  218.0 10.8 collective-permute-done.5
  240.4 6.2 reshape.258
  246.5 8.6 copy.28
  255.2 8.0 fusion.46
  263.1 9.1 fusion.5
  272.3 12.2 fusion.40
  284.4 12.2 fusion.37
  300.5 25.8 %copy.33 = bf16[6,128,3,32,32]{4,3,2,1,0:T(8,128)(2,1)} copy(bf16[6,128,3,32,32]{1,4,3,0,2:T(8,128)(2,1)} %pad_add_fusion) | data formatting | bytes 9437184 | tf_op jit(solution)/shard_map/transpose(jvp())/add_any | solution.py:33
  326.3 24.5 %reshape.259 = bf16[2,3,2,8,8,3072]{5,4,3,2,1,0:T(8,128)(2,1)} reshape(bf16[6,128,3,32,32]{4,3,2,1,0:T(8,128)(2,1)} %copy.33) | data formatting | bytes 9437184 | tf_op jit(solution)/shard_map/transpose(jvp())/reshape;transpose(jvp())/reshape | solution.py:52
  353.7 11.3 fusion.9
  365.9 10.4 fusion.57
  389.9 5.6 reshape.263
  398.8 5.2 fusion.47
  410.6 467.7 %reduce-scatter.5.cloned.1.call-done = f32[8,1024]{1,0:T(8,128)} async-done(((f32[1024,1024]{1,0:T(8,128)}), f32[8,1024]{1,0:T(8,128)}) %reduce-scatter.5.cloned.1.call-update) | async-done | bytes 32784 | tf_op jit(solution)/shard_map/reduce_scatter | solution.py:145
  878.3 654.6 %reduce-scatter.3.cloned.1.call-done = f32[8,3072]{1,0:T(8,128)} async-done(((f32[1024,3072]{1,0:T(8,128)}), f32[8,3072]{1,0:T(8,128)}) %reduce-scatter.3.cloned.1.call-update) | async-done | bytes 98320 | tf_op jit(solution)/shard_map/reduce_scatter | solution.py:144
  (145 shorter events, 108.2 us)
Async XLA Ops:
  7.2 136.0 %copy-start = (bf16[1024,1024]{1,0:T(8,128)(2,1)S(1)}, bf16[1024,1024]{1,0:T(8,128)(2,1)}, u32[]{:S(2)}) copy-start(bf16[1024,1024]{1,0:T(8,128)(2,1)} %param.7) | copy-start | bytes 6291460
  7.2 871.1 %reduce-scatter.5.cloned.1.call-start = ((), (), s32[]{:S(2)}) async-start(), calls=%async_computation.3 | async-start | bytes 4227072 | tf_op jit(solution)/shard_map/reduce_scatter | solution.py:145
  8.6 6.0 collective-permute-start
  15.7 11.6 collective-permute-start.1
  30.2 12.3 copy-start.23
  30.3 12.2 copy-start.27
  32.3 10.3 copy-start.25
  32.4 10.2 copy-start.31
  32.4 10.1 copy-start.29
  111.6 4.7 copy-start.11
  111.7 7.3 copy-start.12
  143.4 8.2 copy-start.22
  147.2 9.5 collective-permute-start.2
  157.5 17.6 %collective-permute-start.3 = (bf16[2,4,24,1024]{3,2,1,0:T(8,128)(2,1)}, bf16[2,4,24,1024]{3,2,1,0:T(8,128)(2,1)S(1)}, u32[]{:S(2)}, u32[]{:S(2)}) collective-permute-start(bf16[2,4,24,1024]{3,2,1,0:T(8,128)(2,1)} %pad_maximum_fusion.5), channel_id=1, source_target_pairs={{16,0},{32,16},{48,32},{64,48},{80,64},{96,80},{112,96},{0,112},{1... | collective-permute-start | bytes 1179656 | tf_op jit(solution)/shard_map/ppermute | solution.py:17
  182.3 4.5 copy-start.2
  211.9 16.9 %copy-start.8 = (bf16[2,16,24,1024]{3,2,1,0:T(8,128)(2,1)S(1)}, bf16[2,16,24,1024]{3,2,1,0:T(8,128)(2,1)}, u32[]{:S(2)}) copy-start(bf16[2,16,24,1024]{3,2,1,0:T(8,128)(2,1)} %reshape.256) | copy-start | bytes 4718596
  213.2 17.3 %copy-start.21 = (bf16[2,2,8,3,8,1024]{5,4,3,2,1,0:T(8,128)(2,1)S(1)}, bf16[2,2,8,3,8,1024]{5,4,3,2,1,0:T(8,128)(2,1)}, u32[]{:S(2)}) copy-start(bf16[2,2,8,3,8,1024]{5,4,3,2,1,0:T(8,128)(2,1)} %copy-done.20) | copy-start | bytes 4718596
  213.2 3.4 collective-permute-start.4
  217.7 11.1 collective-permute-start.5
  238.8 1294.1 %reduce-scatter.3.cloned.1.call-start = ((), (), s32[]{:S(2)}) async-start(), calls=%async_computation.2 | async-start | bytes 12681216 | tf_op jit(solution)/shard_map/reduce_scatter | solution.py:144
  255.2 8.0 copy-start.13
  255.2 8.0 copy-start.17
  284.4 12.2 copy-start.15
  353.7 11.4 copy-start.7
  353.7 11.4 copy-start.26
  353.7 11.4 copy-start.24
  377.0 8.4 copy-start.3
  381.0 16.8 %collective-permute-start.6 = (bf16[2,16,4,1024]{3,2,1,0:T(4,128)(2,1)S(1)}, bf16[2,16,4,1024]{3,2,1,0:T(4,128)(2,1)S(1)}, u32[]{:S(2)}, u32[]{:S(2)}) collective-permute-start(bf16[2,16,4,1024]{3,2,1,0:T(4,128)(2,1)S(1)} %slice.86), channel_id=1, source_target_pairs={{1,0},{2,1},{3,2},{4,3},{5,4},{6,5},{7,6},{8,7},{9,8},{10,9},{11,1... | collective-permute-start | bytes 786440 | tf_op jit(solution)/shard_map/ppermute | solution.py:17
  395.5 3.2 copy-start.18
  397.8 6.2 copy-start.9
  398.8 10.6 collective-permute-start.7
  404.1 1128.8 %copy-start.1 = (bf16[1024,1024]{1,0:T(8,128)(2,1)S(1)}, bf16[1024,1024]{1,0:T(8,128)(2,1)}, u32[]{:S(2)}) copy-start(bf16[1024,1024]{1,0:T(8,128)(2,1)} %param.7) | copy-start | bytes 6291460
  (11 other events, 22.1 us)
Sparse Core Ops, SparseCore 0:
  238.9 639.3 reduce-scatter.4
  881.4 651.4 reduce-scatter.2
where the time goes:
time: 1550 us; the launch traced here: 1540 us
  waiting for transfers between devices  1150 us (74%)
  local copies, waits for them, and re-layouts  201 us (13%)
  matrix products  103 us (7%)
  other arithmetic  50.8 us (3%)
  starting transfers between devices  15.7 us (1%)
    reduce_scatter x1, waiting for transfers between devices, shards(): lax.psum_scatter(qkv_terms, ('lat', 'lon'), scatter_dimension=0, tiled=True)  655 us
    reduce_scatter x1, waiting for transfers between devices, shards(): lax.psum_scatter(out_terms, ('lat', 'lon'), scatter_dimension=0, tiled=True)  468 us
    unnamed x71, local copies, waits for them, and re-layouts  35.7 us
    ppermute x8, waiting for transfers between devices, shifted(): return lax.ppermute(block, axis, route)  32.3 us
  transfers between devices with their start and end apart: 10, of which 8 were waited for; matrix products, arithmetic and copies ran while one was open for 12% of the time, Pallas kernels for 0%

commit v1 on v0

--- a/solution.py
+++ b/solution.py
@@ -1,6 +1,8 @@
 import jax
 import jax.numpy as jnp
 from jax import lax
+from jax.experimental import pallas as pl
+from jax.experimental.pallas import tpu as pltpu
 from jax.sharding import PartitionSpec as P
 
 HEADS = 32
@@ -9,6 +11,160 @@
 
 
 epsilon = 1e-05
+
+
+MESH = pl.DeviceIdType.MESH
+CHUNKS = 4
+LANES = 512
+WIDTH = 256
+
+
+def place():
+    lat, lon = lax.axis_index("lat"), lax.axis_index("lon")
+    return (lat // 4) * 2 + (lon // 2) % 2, lon // 4, lat % 4, lon % 2
+
+
+def device_at(x, y, z, core):
+    return ((x // 2) * 4 + z, y * 4 + (x % 2) * 2 + core)
+
+
+def reduce_kernel(g, qkv_out, out_out, from_core, acc_a, in_a, acc_b, in_b, acc_c, in_c, send, recv):
+    x, y, z, core = place()
+    here = (x, y, z)
+
+    def moved(axis, step):
+        there = list(here)
+        there[axis] = (here[axis] + step) % 4
+        return device_at(there[0], there[1], there[2], core)
+
+    sibling = device_at(x, y, z, 1 - core)
+    barrier = pltpu.get_barrier_semaphore()
+    partners = [sibling] + [moved(axis, step) for axis in range(3) for step in (1, 2, 3)]
+    for partner in partners:
+        pl.semaphore_signal(barrier, inc=1, device_id=partner, device_id_type=MESH)
+    pl.semaphore_wait(barrier, len(partners))
+
+    started = []
+
+    def push(stream, slot, source, target, partner):
+        copy = pltpu.make_async_remote_copy(
+            src_ref=source, dst_ref=target, send_sem=send.at[stream, slot],
+            recv_sem=recv.at[stream, slot], device_id=partner, device_id_type=MESH)
+        copy.start()
+        started.append(copy)
+        return copy
+
+    def run(stream):
+        chunk, part = stream // 2, stream % 2
+        lanes = pl.ds(part * WIDTH, WIDTH)
+        order = [(stream + k) % 3 for k in range(3)]
+        mine = [here[axis] for axis in order]
+        copy = push(stream, 0, g.at[chunk, :, 1 - core, :, lanes], from_core.at[stream], sibling)
+        yield
+        copy.wait_recv()
+
+        def add_block(index, carry):
+            a, b = index // 4, index % 4
+            for c in range(4):
+                at = [None, None, None]
+                for axis, value in zip(order, (a, b, c)):
+                    at[axis] = value
+                row = ((at[0] // 2) * 4 + at[2]) * 8 + at[1] * 2 + at[0] % 2
+                total = g[chunk, row, core, :, lanes].astype(jnp.float32) + from_core[stream, row].astype(jnp.float32)
+                acc_a[stream, a, b * 4 + c] = total.astype(jnp.bfloat16)
+            return carry
+
+        lax.fori_loop(0, 16, add_block, 0)
+        for level, (acc, arrived, blocks) in enumerate(((acc_a, in_a, 16), (acc_b, in_b, 4))):
+            axis, p = order[level], mine[level]
+            half = blocks // 2
+            low, high = pl.ds(0, half), pl.ds(half, half)
+            base = 1 + level * 6
+            right, left = moved(axis, 1), moved(axis, 3)
+            after, before, across = (p + 1) % 4, (p + 3) % 4, (p + 2) % 4
+            relay_up = push(stream, base, acc.at[stream, across, high], arrived.at[stream, 0], right)
+            relay_down = push(stream, base + 1, acc.at[stream, across, low], arrived.at[stream, 1], left)
+            own_up = push(stream, base + 2, acc.at[stream, after, low], arrived.at[stream, 2], right)
+            own_down = push(stream, base + 3, acc.at[stream, before, high], arrived.at[stream, 3], left)
+            yield
+            relay_up.wait_recv()
+            acc[stream, after, high] = (acc[stream, after, high].astype(jnp.float32)
+                                        + arrived[stream, 0].astype(jnp.float32)).astype(jnp.bfloat16)
+            sum_up = push(stream, base + 4, acc.at[stream, after, high], arrived.at[stream, 4], right)
+            relay_down.wait_recv()
+            acc[stream, before, low] = (acc[stream, before, low].astype(jnp.float32)
+                                        + arrived[stream, 1].astype(jnp.float32)).astype(jnp.bfloat16)
+            sum_down = push(stream, base + 5, acc.at[stream, before, low], arrived.at[stream, 5], left)
+            yield
+            own_up.wait_recv()
+            own_down.wait_recv()
+            sum_up.wait_recv()
+            sum_down.wait_recv()
+            total_low = (acc[stream, p, low].astype(jnp.float32) + arrived[stream, 2].astype(jnp.float32)
+                         + arrived[stream, 5].astype(jnp.float32)).astype(jnp.bfloat16)
+            total_high = (acc[stream, p, high].astype(jnp.float32) + arrived[stream, 3].astype(jnp.float32)
+                          + arrived[stream, 4].astype(jnp.float32)).astype(jnp.bfloat16)
+            if level == 0:
+                for i in range(2):
+                    acc_b[stream, i] = total_low[i * 4:i * 4 + 4]
+                    acc_b[stream, i + 2] = total_high[i * 4:i * 4 + 4]
+            else:
+                for i in range(2):
+                    acc_c[stream, i] = total_low[i]
+                    acc_c[stream, i + 2] = total_high[i]
+        axis, p = order[2], mine[2]
+        last = [push(stream, 13 + k, acc_c.at[stream, (p + k + 1) % 4], in_c.at[stream, k], moved(axis, k + 1))
+                for k in range(3)]
+        yield
+        total = acc_c[stream, p].astype(jnp.float32)
+        for k in range(3):
+            last[k].wait_recv()
+            total = total + in_c[stream, k].astype(jnp.float32)
+        columns = WIDTH * chunk
+        if part == 0:
+            qkv_out[:, columns:columns + WIDTH] = total[:8]
+            qkv_out[:, 2048 + columns:2048 + columns + WIDTH] = total[8:]
+        else:
+            qkv_out[:, 1024 + columns:1024 + columns + WIDTH] = total[:8]
+            out_out[:, columns:columns + WIDTH] = total[8:]
+
+    running = [run(stream) for stream in range(2 * CHUNKS)]
+    while running:
+        kept = []
+        for job in running:
+            try:
+                next(job)
+                kept.append(job)
+            except StopIteration:
+                pass
+        running = kept
+    for copy in started:
+        copy.wait_send()
+
+
+def reduce_terms(terms):
+    streams = 2 * CHUNKS
+    bf16 = jnp.bfloat16
+    return pl.pallas_call(
+        reduce_kernel,
+        out_shape=(jax.ShapeDtypeStruct((8, 3072), jnp.float32), jax.ShapeDtypeStruct((8, 1024), jnp.float32)),
+        in_specs=[pl.BlockSpec(memory_space=pltpu.VMEM)],
+        out_specs=(pl.BlockSpec(memory_space=pltpu.VMEM), pl.BlockSpec(memory_space=pltpu.VMEM)),
+        scratch_shapes=[
+            pltpu.VMEM((streams, 64, 16, WIDTH), bf16),
+            pltpu.VMEM((streams, 4, 16, 16, WIDTH), bf16),
+            pltpu.VMEM((streams, 6, 8, 16, WIDTH), bf16),
+            pltpu.VMEM((streams, 4, 4, 16, WIDTH), bf16),
+            pltpu.VMEM((streams, 6, 2, 16, WIDTH), bf16),
+            pltpu.VMEM((streams, 4, 16, WIDTH), bf16),
+            pltpu.VMEM((streams, 3, 16, WIDTH), bf16),
+            pltpu.SemaphoreType.DMA((streams, 16)),
+            pltpu.SemaphoreType.DMA((streams, 16)),
+        ],
+        compiler_params=pltpu.CompilerParams(
+            collective_id=0, has_side_effects=True, vmem_limit_bytes=60 * 1024 * 1024),
+        name="reduce_terms",
+    )(terms)
 
 
 def shifted(block, axis, distance):
@@ -117,11 +273,9 @@
     branch = jnp.dot(mixture_flat, out_weight, preferred_element_type=jnp.float32)
     shifted_out = (framed.reshape(-1, channels).astype(jnp.float32) + branch).astype(jnp.bfloat16)
     shifted_out = shifted_out.reshape(framed.shape)
-    block_out = move_strips(shifted_out, SHIFT, -1)
-    merged, merge_back = jax.vjp(lambda grid_values: merge(grid_values, merge_weight), block_out)
-    block_grad = merge_back(merged_grad)[0]
-    framed_grad_out = move_strips(block_grad, SHIFT, 1)
-    grad_rolled = framed_grad_out.reshape(-1, channels)
+    framed_merged, merge_back = jax.vjp(lambda grid_values: merge(grid_values, merge_weight), shifted_out)
+    grad_rolled = merge_back(move_strips(merged_grad, SHIFT // 2, 1))[0].reshape(-1, channels)
+    merged = move_strips(framed_merged, SHIFT // 2, -1)
     mixture_grad = lax.dot_general(
         grad_rolled, out_weight, (((1,), (1,)), ((), ())), preferred_element_type=jnp.float32
     ).astype(jnp.bfloat16)
@@ -140,10 +294,9 @@
         jnp.bfloat16
     )
     tokens_grad = move_strips(framed_grad.reshape(framed.shape), SHIFT, -1)
-    qkv_weight_grad, out_weight_grad = (
-        lax.psum_scatter(qkv_terms, ("lat", "lon"), scatter_dimension=0, tiled=True),
-        lax.psum_scatter(out_terms, ("lat", "lon"), scatter_dimension=0, tiled=True),
-    )
+    terms = jnp.concatenate([qkv_terms, out_terms], axis=1).astype(jnp.bfloat16)
+    terms = terms.reshape(64, 2, 8, 2, 2, 4, 256).transpose(5, 0, 1, 3, 2, 4, 6).reshape(4, 64, 2, 16, 512)
+    qkv_weight_grad, out_weight_grad = reduce_terms(terms)
     return (merged, tokens_grad, qkv_weight_grad, out_weight_grad)
 
 

time: 1550 us -> 437 us (0.28)
  waiting for transfers between devices: 1150 us -> 17 us
  Pallas kernels: 0 us -> 36.3 us
    reduce_scatter x2 -> x0, waiting for transfers between devices: 1120 us -> none  [the longest x1 655 us: shards(): lax.psum_scatter(qkv_terms, ('lat', 'lon'), scatter_dimension=0, tiled=True)]
    pallas_call x0 -> x1, Pallas kernels: none -> 36.3 us  [reduce_terms(): pl.pallas_call(reduce_kernel, out_shape=(jax.ShapeDtypeStruct((8, 3072),...]
    unnamed x71 -> x56, local copies, waits for them, and re-layouts: 35.7 us -> 31.7 us
  transfers between devices with their start and end apart: 10 -> 8, of which waited for: 8 -> 3; matrix products, arithmetic and copies ran while one was open for 12% -> 12% of each run, Pallas kernels for 0% -> 8%
where the time goes in v1:
time: 437 us; the launch traced here: 432 us
  local copies, waits for them, and re-layouts  200 us (46%)
  matrix products  105 us (24%)
  other arithmetic  53.9 us (12%)
  Pallas kernels  36.3 us (8%)
  starting transfers between devices  18.4 us (4%)
  waiting for transfers between devices  17 us (4%)
    pallas_call x1, Pallas kernels, reduce_terms(): pl.pallas_call(reduce_kernel, out_shape=(jax.ShapeDtypeStruct((8, 3072),...  36.3 us
    unnamed x56, local copies, waits for them, and re-layouts  31.7 us
    dot_general x3, matrix products, window_attention(): jnp.einsum('bqhd,bkhd->bhqk', queries, keys_part, preferred_element_type=...  26.7 us
    add_any x1, local copies, waits for them, and re-layouts, window_attention(): queries = pieces[:, :, 0]  25.8 us
    reshape x1, local copies, waits for them, and re-layouts, to_windows(): blocks.reshape(lat_rows // WIN * (lon_cols // WIN), lev_count * WIN * WIN...  24.9 us
    dot_general x3, matrix products, window_attention(): jnp.einsum('bhqk,bkhd->bqhd', attention, values_part, preferred_element_t...  23.3 us
    reshape x1, local copies, waits for them, and re-layouts, window_attention(): pieces = window_values.reshape(windows, places, 3, HEADS, head_dim)  21.3 us
    ppermute x8, starting transfers between devices, shifted(): return lax.ppermute(block, axis, route)  18.4 us
  transfers between devices with their start and end apart: 8, of which 3 were waited for; matrix products, arithmetic and copies ran while one was open for 12% of the time, Pallas kernels for 8%

profile of v1, /device:TPU:1, one launch (start us, length us, event | category | flops | bytes accessed | tf_op | source)
XLA Modules:
  0.0 431.7 jit_solution(576861273321604281)
XLA Ops:
  11.5 6.1 %collective-permute-done.5 = bf16[2,2,12,1024]{3,1,2,0:T(2,128)(2,1)S(1)} collective-permute-done((bf16[2,2,12,1024]{3,1,2,0:T(2,128)(2,1)S(1)}, bf16[2,2,12,1024]{3,1,2,0:T(2,128)(2,1)S(1)}, u32[]{:S(2)}, u32[]{:S(2)}) %collective-permute-start.5) | collective-permute-done | bytes 98336 | tf_op jit(solution)/shard_map/ppermute | solution.py:173
  20.3 8.0 %fusion.8 = f32[192,4096]{1,0:T(8,128)} fusion(bf16[192,1024]{1,0:T(8,128)(2,1)S(1)} %reshape.253, bf16[4096,1024]{1,0:T(8,128)(2,1)} %param.8), kind=kOutput, calls=%fused_computation.16 | convolution fusion | flops 1612185600 | bytes 11927552 | tf_op jit(solution)/shard_map/transpose(jvp())/dot_general | solution.py:232
  28.3 5.6 %reshape.262 = f32[2,8,12,2,2,1024]{5,4,3,2,1,0:T(2,128)} reshape(f32[192,4096]{1,0:T(8,128)} %fusion.8) | data formatting | bytes 6291456 | tf_op jit(solution)/shard_map/transpose(jvp())/convert_element_type | solution.py:180
  40.9 8.0 %convolution_convert_fusion.1 = bf16[768,3072]{1,0:T(8,128)(2,1)S(1)} fusion(bf16[768,1024]{1,0:T(8,128)(2,1)S(1)} %fusion.19, bf16[1024,3072]{1,0:T(8,128)(2,1)} %param.6), kind=kOutput, calls=%fused_computation.14 | convolution fusion | flops 4834197504 | bytes 12582912 | tf_op jit(solution)/shard_map/dot_general | solution.py:263
  51.5 21.3 %reshape.249 = bf16[6,128,3,32,32]{4,3,2,1,0:T(8,128)(2,1)} reshape(bf16[2,3,2,8,8,3072]{5,4,3,2,1,0:T(8,128)(2,1)} %bitcast.121) | data formatting | bytes 9437184 | tf_op jit(solution)/shard_map/jvp()/reshape;jvp()/reshape | solution.py:188
  72.8 14.3 %fusion.56 = (bf16[6,128,1,32,32]{4,3,2,1,0:T(8,128)(2,1)}, bf16[6,128,1,32,32]{4,3,2,1,0:T(8,128)(2,1)}, bf16[6,128,1,32,32]{4,3,2,1,0:T(8,128)(2,1)}) fusion(bf16[6,128,3,32,32]{4,3,2,1,0:T(8,128)(2,1)} %reshape.249), kind=kLoop, calls=%fused_computation.105 | loop fusion | bytes 9437184 | tf_op jit(solution)/shard_map/jvp()/slice | solution.py:191
  87.1 8.6 %copy.49 = bf16[6,128,1,32,32]{1,4,3,0,2:T(8,128)(2,1)} copy(bf16[6,128,1,32,32]{4,3,2,1,0:T(8,128)(2,1)} %get-tuple-element.19) | data formatting | bytes 3145728
  95.7 9.1 %copy.50 = bf16[6,128,1,32,32]{1,4,3,0,2:T(8,128)(2,1)} copy(bf16[6,128,1,32,32]{4,3,2,1,0:T(8,128)(2,1)} %get-tuple-element.20) | data formatting | bytes 3145728
  109.9 5.7 %divide_convert_fusion = bf16[6,32,128,128]{2,3,1,0:T(8,128)(2,1)} fusion(f32[6,32,128,128]{2,3,1,0:T(8,128)S(1)} %get-tuple-element.28, f32[6,32,128]{2,1,0:T(8,128)S(1)} %get-tuple-element.27, pred[6,128,128]{1,2,0:T(8,128)(4,1)S(1)} %broadcast_compare_fusion), kind=kLoop, calls=%fused_computation.8 | loop fusion | flops 12582912 | bytes 19070976 | tf_op jit(solution)/shard_map/jvp()/convert_element_type | solution.py:197
  116.3 8.6 %copy.48 = bf16[6,128,1,32,32]{1,4,3,0,2:T(8,128)(2,1)} copy(bf16[6,128,1,32,32]{4,3,2,1,0:T(8,128)(2,1)} %get-tuple-element.18) | data formatting | bytes 3145728
  124.9 6.2 %fusion.43 = bf16[6,128,32,32]{1,3,2,0:T(8,128)(2,1)} fusion(bf16[6,32,128,128]{2,3,1,0:T(8,128)(2,1)} %divide_convert_fusion, bf16[6,128,1,32,32]{1,4,3,0,2:T(8,128)(2,1)} %copy.48), kind=kOutput, calls=%fused_computation.76 | convolution fusion | flops 202113024 | bytes 9437184 | tf_op jit(solution)/shard_map/jvp(bhqk,bkhd->bqhd)/dot_general | solution.py:198
  131.1 9.9 %copy.26 = bf16[6,128,32,32]{3,2,1,0:T(8,128)(2,1)} copy(bf16[6,128,32,32]{1,3,2,0:T(8,128)(2,1)} %fusion.43) | data formatting | bytes 3145728 | tf_op jit(solution)/shard_map/jvp()/convert_element_type | solution.py:201
  141.0 9.7 %reshape.250 = bf16[2,3,2,8,8,1024]{5,4,3,2,1,0:T(8,128)(2,1)} reshape(bf16[6,128,32,32]{3,2,1,0:T(8,128)(2,1)} %copy.26) | data formatting | bytes 3145728 | tf_op jit(solution)/shard_map/jvp()/reshape;jvp()/reshape | solution.py:213
  157.0 5.3 %reshape.264 = f32[2,8,2,12,2,1024]{5,4,3,2,1,0:T(2,128)} reshape(f32[768,1024]{1,0:T(8,128)} %fusion.24) | data formatting | bytes 6291456 | tf_op jit(solution)/shard_map/jvp()/convert_element_type | solution.py:177
  165.3 6.0 %multiply_reduce_fusion.1 = (f32[2,8,12]{2,1,0:T(8,128)S(1)}, f32[2,8,12]{2,1,0:T(8,128)S(1)}) fusion(f32[2,8,12,2,2,1024]{5,4,3,2,1,0:T(2,128)} %reshape.262, f32[2,8,12]{2,1,0:T(8,128)S(1)} %broadcast_multiply_fusion.1, f32[2,8,2,12,2,1024]{5,4,3,2,1,0:T(2,128)S(1)} %copy-done.2), kind=kLoop, calls=%fused_computation.44 | loop fusion | flops 3931776 | bytes 6293760 | tf_op jit(solution)/shard_map/transpose(jvp())/reduce_sum | solution.py:180
  177.0 8.7 %fusion.36 = bf16[2,8,2,12,2,1024]{5,4,3,2,1,0:T(2,128)(2,1)} fusion(f32[2,8,12]{2,1,0:T(8,128)S(1)} %add_multiply_fusion, f32[2,8,12]{2,1,0:T(8,128)S(1)} %get-tuple-element.25, f32[2,8,12]{2,1,0:T(8,128)S(1)} %get-tuple-element.26, f32[2,8,12,2,2,1024]{5,4,3,2,1,0:T(2,128)} %reshape.262, f32[2,8,12]{2,1,0:T(8,128)S(1)} %broadcast_multiply_fusion.1, ...), kind=kLoop, calls=%fused_computation.73 | loop fusion | flops 4718592 | bytes 7867392 | tf_op jit(solution)/shard_map/transpose(jvp())/transpose | solution.py:228
  192.7 6.1 %reshape.255 = bf16[6,128,32,32]{3,2,1,0:T(8,128)(2,1)} reshape(bf16[2,3,2,8,8,1024]{5,4,3,2,1,0:T(8,128)(2,1)S(1)} %bitcast.128) | data formatting | bytes 3145728 | tf_op jit(solution)/shard_map/transpose(jvp())/reshape;transpose(jvp())/reshape | solution.py:201
  198.9 8.6 %copy.33 = bf16[6,32,32,128]{3,2,1,0:T(8,128)(2,1)} copy(bf16[6,32,32,128]{2,1,3,0:T(8,128)(2,1)} %bitcast.120) | data formatting | bytes 3145728 | tf_op jit(solution)/shard_map/transpose(jvp(bhqk,bkhd->bqhd))/transpose | solution.py:198
  207.5 7.9 %fusion.46 = bf16[6,128,1,32,32]{1,4,3,0,2:T(8,128)(2,1)} fusion(bf16[6,32,32,128]{3,2,1,0:T(8,128)(2,1)} %copy.33, bf16[6,32,128,128]{2,3,1,0:T(8,128)(2,1)} %divide_convert_fusion), kind=kOutput, calls=%fused_computation.77 | convolution fusion | flops 202113024 | bytes 9437184 | tf_op jit(solution)/shard_map/transpose(jvp(bhqk,bkhd->bqhd))/dot_general | solution.py:198
  215.5 9.1 %fusion.5 = (f32[6,32,128]{2,1,0:T(8,128)S(1)}, bf16[6,32,128,128]{2,3,1,0:T(8,128)(2,1)}) fusion(f32[6,32,128,128]{2,3,1,0:T(8,128)} %copy-done.8, f32[6,32,128]{2,1,0:T(8,128)S(1)} %multiply_divide_fusion, pred[6,128,128]{1,2,0:T(8,128)(4,1)S(1)} %broadcast_compare_fusion, bf16[6,32,32,128]{3,2,1,0:T(8,128)(2,1)S(1)} %copy-done.12, ...), kind=kOutput, calls=%fused_computation.7 | convolution fusion | flops 223322112 | bytes 22315008 | tf_op jit(solution)/shard_map/transpose(jvp(bhqk,bkhd->bqhd))/dot_general | solution.py:198
  224.6 12.2 %fusion.37 = bf16[6,128,1,32,32]{1,4,3,0,2:T(8,128)(2,1)} fusion(bf16[6,128,1,32,32]{1,4,3,0,2:T(8,128)(2,1)} %copy.49, bf16[6,32,128,128]{2,3,1,0:T(8,128)(2,1)} %get-tuple-element.30, f32[6,32,128,128]{2,3,1,0:T(8,128)} %copy-done.8, f32[6,32,128]{2,1,0:T(8,128)S(1)} %neg.25, f32[6,32,128]{2,1,0:T(8,128)S(1)} %get-tuple-element.27, ...), kind=kOutput, calls=%fused_computation.74 | convolution fusion | flops 224133120 | bytes 22315008 | tf_op jit(solution)/shard_map/transpose(jvp(bqhd,bkhd->bhqk))/dot_general | solution.py:192
  236.8 9.5 %fusion.40 = bf16[6,128,1,32,32]{1,4,3,0,2:T(8,128)(2,1)} fusion(bf16[6,128,1,32,32]{1,4,3,0,2:T(8,128)(2,1)S(1)} %copy-done.16, bf16[6,32,128,128]{2,3,1,0:T(8,128)(2,1)} %get-tuple-element.30, f32[6,32,128,128]{2,3,1,0:T(8,128)} %copy-done.8, f32[6,32,128]{2,1,0:T(8,128)S(1)} %neg.25, f32[6,32,128]{2,1,0:T(8,128)S(1)} %get-tuple-element.27, ...), kind=kOutput, calls=%fused_computation.75 | convolution fusion | flops 224133120 | bytes 22315008 | tf_op jit(solution)/shard_map/transpose(jvp(bqhd,bkhd->bhqk))/dot_general | solution.py:192
  255.4 25.8 %copy.38 = bf16[6,128,3,32,32]{4,3,2,1,0:T(8,128)(2,1)} copy(bf16[6,128,3,32,32]{1,4,3,0,2:T(8,128)(2,1)} %pad_add_fusion) | data formatting | bytes 9437184 | tf_op jit(solution)/shard_map/transpose(jvp())/add_any | solution.py:189
  281.1 24.9 %reshape.256 = bf16[2,3,2,8,8,3072]{5,4,3,2,1,0:T(8,128)(2,1)} reshape(bf16[6,128,3,32,32]{4,3,2,1,0:T(8,128)(2,1)} %copy.38) | data formatting | bytes 9437184 | tf_op jit(solution)/shard_map/transpose(jvp())/reshape;transpose(jvp())/reshape | solution.py:208
  309.0 11.3 %fusion.9 = (f32[768]{0:T(1024)S(1)}, f32[768]{0:T(1024)S(1)}, bf16[768,1024]{1,0:T(8,128)(2,1)}) fusion(f32[768]{0:T(1024)S(1)} %rsqrt.28, f32[768]{0:T(1024)S(1)} %div.62, bf16[2,16,24,1024]{3,2,1,0:T(8,128)(2,1)S(1)} %copy-done.5, bf16[768,3072]{1,0:T(8,128)(2,1)S(1)} %bitcast.129, bf16[1024,3072]{1,0:T(8,128)(2,1)} %param.6), kind=kOutput, calls=%fused_computation.21 | convolution fusion | flops 4838127616 | bytes 14168064 | tf_op jit(solution)/shard_map/dot_general | solution.py:289
  321.2 9.4 %convolution_convert_fusion = bf16[1024,3072]{1,0:T(8,128)(2,1)} fusion(bf16[768,1024]{1,0:T(8,128)(2,1)S(1)} %bitcast.134, bf16[768,3072]{1,0:T(8,128)(2,1)} %bitcast.130), kind=kOutput, calls=%fused_computation.13 | convolution fusion | flops 4834983936 | bytes 12582912 | tf_op jit(solution)/shard_map/dot_general | solution.py:286
  343.9 5.8 %reshape.261 = f32[192,4096]{1,0:T(8,128)} reshape(f32[2,8,12,2,2,1024]{5,4,3,2,1,0:T(2,128)} %copy.28) | data formatting | bytes 6291456 | tf_op jit(solution)/shard_map/jvp()/convert_element_type | solution.py:177
  349.7 6.3 %fusion.47 = bf16[192,1024]{1,0:T(8,128)(2,1)S(1)} fusion(bf16[4096,1024]{1,0:T(8,128)(2,1)} %param.8, f32[192,4096]{1,0:T(8,128)} %reshape.261, f32[192]{0:T(256)S(1)} %rsqrt.30, f32[192]{0:T(256)S(1)} %div.67), kind=kOutput, calls=%fused_computation.78 | convolution fusion | flops 1613168640 | bytes 11929088 | tf_op jit(solution)/shard_map/jvp()/dot_general | solution.py:232
  356.0 6.9 %pad_maximum_fusion = bf16[1024,4096]{1,0:T(8,128)(2,1)} fusion(bf16[1024,1024]{1,0:T(8,128)(2,1)S(1)} %copy-done.14, bf16[1024,3072]{1,0:T(8,128)(2,1)} %convolution_convert_fusion), kind=kLoop, calls=%fused_computation.11 | loop fusion | flops 16777216 | bytes 16777216 | tf_op jit(solution)/shard_map/concatenate | solution.py:297
  365.4 8.1 %copy.41 = bf16[64,2,8,2,2,4,256]{6,2,4,3,1,0,5:T(8,128)(2,1)} copy(bf16[64,2,8,2,2,4,256]{6,2,5,4,3,1,0:T(8,128)(2,1)} %bitcast.118) | data formatting | bytes 16777216 | tf_op jit(solution)/shard_map/convert_element_type | solution.py:297
  373.4 36.3 %reduce_terms.1 = (f32[8,3072]{1,0:T(8,128)}, f32[8,1024]{1,0:T(8,128)}) custom-call(bf16[4,64,2,16,512]{4,3,2,1,0:T(8,128)(2,1)} %bitcast.119), custom_call_target="tpu_custom_call" | custom-call | tf_op jit(solution)/shard_map/reduce_terms/pallas_call | solution.py:148
  419.1 8.6 %collective-permute-done.3 = bf16[2,2,12,1024]{3,2,1,0:T(8,128)(2,1)S(1)} collective-permute-done((bf16[2,2,12,1024]{3,2,1,0:T(8,128)(2,1)S(1)}, bf16[2,2,12,1024]{3,2,1,0:T(8,128)(2,1)S(1)}, u32[]{:S(2)}, u32[]{:S(2)}) %collective-permute-start.3) | collective-permute-done | bytes 98336 | tf_op jit(solution)/shard_map/ppermute | solution.py:173
  (128 shorter events, 92.3 us)
Async XLA Ops:
  0.6 152.8 %copy-start = (bf16[1024,1024]{1,0:T(8,128)(2,1)S(1)}, bf16[1024,1024]{1,0:T(8,128)(2,1)}, u32[]{:S(2)}) copy-start(bf16[1024,1024]{1,0:T(8,128)(2,1)} %param.7) | copy-start | bytes 6291460
  2.7 15.4 %collective-permute-start = (bf16[2,16,4,1024]{3,2,1,0:T(4,128)(2,1)}, bf16[2,16,4,1024]{3,2,1,0:T(4,128)(2,1)S(1)}, u32[]{:S(2)}, u32[]{:S(2)}) collective-permute-start(bf16[2,16,4,1024]{3,2,1,0:T(4,128)(2,1)} %slice.57), channel_id=1, source_target_pairs={{15,0},{0,1},{1,2},{2,3},{3,4},{4,5},{5,6},{6,7},{7,8},{8,9},{9,10... | collective-permute-start | bytes 786440 | tf_op jit(solution)/shard_map/ppermute | solution.py:173
  6.1 3.4 collective-permute-start.4
  9.6 8.0 %collective-permute-start.5 = (bf16[2,2,12,1024]{3,1,2,0:T(2,128)(2,1)S(1)}, bf16[2,2,12,1024]{3,1,2,0:T(2,128)(2,1)S(1)}, u32[]{:S(2)}, u32[]{:S(2)}) collective-permute-start(bf16[2,2,12,1024]{3,1,2,0:T(2,128)(2,1)S(1)} %pad_maximum_fusion.8), channel_id=1, source_target_pairs={{112,0},{0,16},{16,32},{32,48},{48,64},{64,80},{80,96},{96,112},{1... | collective-permute-start | bytes 294920 | tf_op jit(solution)/shard_map/ppermute | solution.py:173
  20.0 13.9 %collective-permute-start.1 = (bf16[2,4,24,1024]{3,2,1,0:T(8,128)(2,1)}, bf16[2,4,24,1024]{3,2,1,0:T(8,128)(2,1)S(1)}, u32[]{:S(2)}, u32[]{:S(2)}) collective-permute-start(bf16[2,4,24,1024]{3,2,1,0:T(8,128)(2,1)} %pad_maximum_fusion.6), channel_id=1, source_target_pairs={{112,0},{0,16},{16,32},{32,48},{48,64},{64,80},{80,96},{96,112},{1... | collective-permute-start | bytes 1179656 | tf_op jit(solution)/shard_map/ppermute | solution.py:173
  36.8 12.1 %copy-start.17 = (f32[2,16,24]{2,1,0:T(8,128)}, f32[2,16,24]{2,1,0:T(8,128)S(1)}, u32[]{:S(2)}) copy-start(f32[2,16,24]{2,1,0:T(8,128)S(1)} %broadcast_multiply_fusion) | copy-start | bytes 9220
  38.9 10.0 %copy-start.19 = (f32[2,16,24]{2,1,0:T(8,128)}, f32[2,16,24]{2,1,0:T(8,128)S(1)}, u32[]{:S(2)}) copy-start(f32[2,16,24]{2,1,0:T(8,128)S(1)} %fusion.20) | copy-start | bytes 9220
  39.0 9.9 %copy-start.22 = (f32[768]{0:T(1024)}, f32[768]{0:T(1024)S(1)}, u32[]{:S(2)}) copy-start(f32[768]{0:T(1024)S(1)} %add.48) | copy-start | bytes 9220
  109.9 6.4 %copy-start.8 = (f32[6,32,128,128]{2,3,1,0:T(8,128)}, f32[6,32,128,128]{2,3,1,0:T(8,128)S(1)}, u32[]{:S(2)}) copy-start(f32[6,32,128,128]{2,3,1,0:T(8,128)S(1)} %get-tuple-element.28) | copy-start | bytes 37748740
  150.6 2.8 copy-start.4
  152.3 1.2 copy-start.15
  162.3 2.9 copy-start.2
  207.5 8.0 %copy-start.9 = (bf16[6,128,1,32,32]{1,4,3,0,2:T(8,128)(2,1)S(1)}, bf16[6,128,1,32,32]{1,4,3,0,2:T(8,128)(2,1)}, u32[]{:S(2)}) copy-start(bf16[6,128,1,32,32]{1,4,3,0,2:T(8,128)(2,1)} %copy.48) | copy-start | bytes 4718596
  207.5 8.0 %copy-start.12 = (bf16[6,32,32,128]{3,2,1,0:T(8,128)(2,1)S(1)}, bf16[6,32,32,128]{3,2,1,0:T(8,128)(2,1)}, u32[]{:S(2)}) copy-start(bf16[6,32,32,128]{3,2,1,0:T(8,128)(2,1)} %copy.33) | copy-start | bytes 4718596
  224.6 12.2 %copy-start.16 = (bf16[6,128,1,32,32]{1,4,3,0,2:T(8,128)(2,1)S(1)}, bf16[6,128,1,32,32]{1,4,3,0,2:T(8,128)(2,1)}, u32[]{:S(2)}) copy-start(bf16[6,128,1,32,32]{1,4,3,0,2:T(8,128)(2,1)} %copy.50) | copy-start | bytes 4718596
  246.3 5.4 %copy-start.11 = (bf16[6,128,1,32,32]{1,4,3,0,2:T(8,128)(2,1)S(1)}, bf16[6,128,1,32,32]{1,4,3,0,2:T(8,128)(2,1)}, u32[]{:S(2)}) copy-start(bf16[6,128,1,32,32]{1,4,3,0,2:T(8,128)(2,1)} %fusion.46) | copy-start | bytes 4718596
  306.1 2.9 copy-start.5
  308.9 11.4 %copy-start.13 = (bf16[2,2,8,3,8,3072]{5,4,3,2,1,0:T(8,128)(2,1)}, bf16[2,2,8,3,8,3072]{5,4,3,2,1,0:T(8,128)(2,1)S(1)}, u32[]{:S(2)}) copy-start(bf16[2,2,8,3,8,3072]{5,4,3,2,1,0:T(8,128)(2,1)S(1)} %copy.39) | copy-start | bytes 14155780
  309.0 11.4 %copy-start.20 = (f32[2,16,24]{2,1,0:T(8,128)S(1)}, f32[2,16,24]{2,1,0:T(8,128)}, u32[]{:S(2)}) copy-start(f32[2,16,24]{2,1,0:T(8,128)} %copy-done.19) | copy-start | bytes 9220
  309.0 11.5 %copy-start.18 = (f32[2,16,24]{2,1,0:T(8,128)S(1)}, f32[2,16,24]{2,1,0:T(8,128)}, u32[]{:S(2)}) copy-start(f32[2,16,24]{2,1,0:T(8,128)} %copy-done.17) | copy-start | bytes 9220
  321.2 9.5 %copy-start.23 = (f32[768]{0:T(1024)S(1)}, f32[768]{0:T(1024)}, u32[]{:S(2)}) copy-start(f32[768]{0:T(1024)} %copy-done.22) | copy-start | bytes 9220
  330.7 8.8 %copy-start.3 = (f32[2,8,2,12,2,1024]{5,4,3,2,1,0:T(2,128)S(1)}, f32[2,8,2,12,2,1024]{5,4,3,2,1,0:T(2,128)}, u32[]{:S(2)}) copy-start(f32[2,8,2,12,2,1024]{5,4,3,2,1,0:T(2,128)} %reshape.264) | copy-start | bytes 9437188
  334.8 77.9 %collective-permute-start.6 = (bf16[2,16,4,1024]{3,2,1,0:T(4,128)(2,1)S(1)}, bf16[2,16,4,1024]{3,2,1,0:T(4,128)(2,1)S(1)}, u32[]{:S(2)}, u32[]{:S(2)}) collective-permute-start(bf16[2,16,4,1024]{3,2,1,0:T(4,128)(2,1)S(1)} %slice.84), channel_id=1, source_target_pairs={{1,0},{2,1},{3,2},{4,3},{5,4},{6,5},{7,6},{8,7},{9,8},{10,9},{11,1... | collective-permute-start | bytes 786440 | tf_op jit(solution)/shard_map/ppermute | solution.py:173
  349.7 6.3 %copy-start.14 = (bf16[1024,1024]{1,0:T(8,128)(2,1)S(1)}, bf16[1024,1024]{1,0:T(8,128)(2,1)}, u32[]{:S(2)}) copy-start(bf16[1024,1024]{1,0:T(8,128)(2,1)} %convolution_convert_fusion.4) | copy-start | bytes 6291460
  365.0 47.6 %copy-start.6 = (bf16[2,16,20,1024]{3,2,1,0:T(8,128)(2,1)}, bf16[2,16,20,1024]{3,2,1,0:T(8,128)(2,1)S(1)}, u32[]{:S(2)}) copy-start(bf16[2,16,20,1024]{3,2,1,0:T(8,128)(2,1)S(1)} %slice.83) | copy-start | bytes 3932164
  409.8 6.6 %collective-permute-start.2 = (bf16[2,8,2,1024]{3,2,1,0:T(2,128)(2,1)S(1)}, bf16[2,8,2,1024]{3,2,1,0:T(2,128)(2,1)S(1)}, u32[]{:S(2)}, u32[]{:S(2)}) collective-permute-start(bf16[2,8,2,1024]{3,2,1,0:T(2,128)(2,1)S(1)} %slice.80), channel_id=1, source_target_pairs={{1,0},{2,1},{3,2},{4,3},{5,4},{6,5},{7,6},{8,7},{9,8},{10,9},{11,1... | collective-permute-start | bytes 196616 | tf_op jit(solution)/shard_map/ppermute | solution.py:173
  412.7 16.1 %copy-start.7 = (bf16[2,16,20,1024]{3,2,1,0:T(8,128)(2,1)S(1)}, bf16[2,16,20,1024]{3,2,1,0:T(8,128)(2,1)}, u32[]{:S(2)}) copy-start(bf16[2,16,20,1024]{3,2,1,0:T(8,128)(2,1)} %copy-done.6) | copy-start | bytes 3932164
  412.7 16.3 %collective-permute-start.7 = (bf16[2,4,24,1024]{3,2,1,0:T(8,128)(2,1)S(1)}, bf16[2,4,24,1024]{3,2,1,0:T(8,128)(2,1)S(1)}, u32[]{:S(2)}, u32[]{:S(2)}) collective-permute-start(bf16[2,4,24,1024]{3,2,1,0:T(8,128)(2,1)S(1)} %pad_maximum_fusion.4), channel_id=1, source_target_pairs={{16,0},{32,16},{48,32},{64,48},{80,64},{96,80},{112,96},{0,112},{1... | collective-permute-start | bytes 1179656 | tf_op jit(solution)/shard_map/ppermute | solution.py:173
  416.4 11.3 %collective-permute-start.3 = (bf16[2,2,12,1024]{3,2,1,0:T(8,128)(2,1)S(1)}, bf16[2,2,12,1024]{3,2,1,0:T(8,128)(2,1)S(1)}, u32[]{:S(2)}, u32[]{:S(2)}) collective-permute-start(bf16[2,2,12,1024]{3,2,1,0:T(8,128)(2,1)S(1)} %pad_maximum_fusion.7), channel_id=1, source_target_pairs={{16,0},{32,16},{48,32},{64,48},{80,64},{96,80},{112,96},{0,112},{1... | collective-permute-start | bytes 294920 | tf_op jit(solution)/shard_map/ppermute | solution.py:173
  427.8 3.8 copy-start.1
  428.7 1.5 copy-start.21
  428.7 2.2 copy-start.24
  (1 other events, 1.1 us)

commit v2 on v1

v2 whole, which is shorter than its diff:
```python
import jax
import jax.numpy as jnp
import numpy as np
from jax import lax
from jax.experimental import pallas as pl
from jax.experimental.pallas import tpu as pltpu
from jax.sharding import PartitionSpec as P

SHIFT = 4
F32, BF16 = jnp.float32, jnp.bfloat16
epsilon = 1e-05
SCALE = 32 ** -0.5
MIB = 1024 * 1024
NT = (((1,), (1,)), ((), ()))
TN = (((0,), (0,)), ((), ()))


def params(limit=60):
    return pltpu.CompilerParams(vmem_limit_bytes=limit * MIB)


def dot(left, right, dims=(((1,), (0,)), ((), ()))):
    return lax.dot_general(left, right, dims, preferred_element_type=F32)


def window_order():
    t = np.arange(128)
    quarter, level, a, b = t // 32, t // 16 % 2, t // 4 % 4, t % 4
    natural = (level * 8 + 2 * a + quarter % 2) * 8 + 2 * b + quarter // 2
    return (natural[:, None] == t[None, :]).astype(np.float32)


def statistics(values):
    center = jnp.mean(values, axis=-1, keepdims=True)
    shifted_values = values - center
    spread = jnp.mean(jnp.square(shifted_values), axis=-1, keepdims=True)
    return shifted_values, lax.rsqrt(spread + epsilon)


def prepare_kernel(framed, order, x_out, normed_out, normed_turned):
    natural = framed[...].astype(F32).reshape(128, 1024).astype(BF16)
    values = dot(order[...], natural)
    x_out[...] = values.astype(BF16)
    centered, inverse = statistics(values)
    normed = centered * inverse
    normed_out[...] = normed.astype(BF16)
    normed_turned[...] = normed.T.astype(BF16)


def prepare(framed, order):
    return pl.pallas_call(
        prepare_kernel,
        grid=(6,),
        out_shape=(jax.ShapeDtypeStruct((768, 1024), BF16), jax.ShapeDtypeStruct((768, 1024), BF16),
                   jax.ShapeDtypeStruct((1024, 768), BF16)),
        in_specs=[pl.BlockSpec((2, 8, 8, 1024), lambda w: (0, w // 3, w % 3, 0)),
                  pl.BlockSpec((128, 128), lambda w: (0, 0))],
        out_specs=(pl.BlockSpec((128, 1024), lambda w: (w, 0)), pl.BlockSpec((128, 1024), lambda w: (w, 0)),
                   pl.BlockSpec((1024, 128), lambda w: (0, w))),
        compiler_params=params(), name="prepare",
    )(framed, order)


def head_masks(rows):
    lane = lax.broadcasted_iota(jnp.int32, (rows, 128), 1)
    return [lane // 32 == head for head in range(4)]


def spread_heads(values, masks):
    zero = jnp.zeros_like(values)
    return jnp.concatenate([jnp.where(mask, values, zero) for mask in masks], axis=0)


def edge_marks(edge):
    row = (lax.broadcasted_iota(jnp.int32, (128, 1), 0) // 4 % 4 < 2) & edge
    column = (lax.broadcasted_iota(jnp.int32, (1, 512), 1) // 4 % 4 < 2) & edge
    return row.astype(jnp.int32) != column.astype(jnp.int32)


def attend_kernel(normed, wq, wk, wv, q_out, k_out, v_out, p_out, mix_out, mix_turned):
    for out, weight in ((q_out, wq), (k_out, wk), (v_out, wv)):
        out[...] = dot(normed[...], weight[...]).astype(BF16)
    masks = head_masks(128)
    edge = lax.axis_index("lat") == 0

    def column(wb, carry):
        for wa in range(2):
            w = wa * 3 + wb
            rows = pl.ds(pl.multiple_of(w * 128, 128), 128)
            for group in range(2):
                lanes = pl.ds(group * 128, 128)
                queries, keys, values = q_out[rows, lanes], k_out[rows, lanes], v_out[rows, lanes]
                scores = dot(queries, spread_heads(keys, masks), NT)
                weights = jnp.exp(scores * SCALE)
                if wa == 0:
                    weights = jnp.where(edge_marks(edge), 0.0, weights)
                pieces = []
                for head in range(4):
                    piece = weights[:, head * 128:head * 128 + 128]
                    pieces.append(piece * (1.0 / jnp.sum(piece, axis=-1, keepdims=True)))
                attention = jnp.concatenate(pieces, axis=1).astype(BF16)
                p_out[w, group] = attention
                mixture = dot(attention, spread_heads(values, masks))
                mix_out[rows, lanes] = mixture.astype(BF16)
                mix_turned[lanes, rows] = mixture.T.astype(BF16)
        return carry

    lax.fori_loop(0, 3, column, 0)


def attend(normed, qkv_weight):
    tokens = jax.ShapeDtypeStruct((768, 1024), BF16)
    block = pl.BlockSpec((768, 256), lambda c: (0, c))
    weight = lambda third: pl.BlockSpec((1024, 256), lambda c: (0, third * 4 + c))
    return pl.pallas_call(
        attend_kernel,
        grid=(4,),
        out_shape=(tokens, tokens, tokens, jax.ShapeDtypeStruct((6, 8, 128, 512), BF16), tokens,
                   jax.ShapeDtypeStruct((1024, 768), BF16)),
        in_specs=[pl.BlockSpec((768, 1024), lambda c: (0, 0)), weight(0), weight(1), weight(2)],
        out_specs=(block, block, block, pl.BlockSpec((6, 2, 128, 512), lambda c: (0, c, 0, 0)), block,
                   pl.BlockSpec((256, 768), lambda c: (c, 0))),
        compiler_params=params(), name="attend",
    )(normed, qkv_weight, qkv_weight, qkv_weight)


def merge_kernel(x, mixture, merged_grad, out_weight, merge_weight, merged_out, grad_out, mixture_grad,
                 normed, total, normed_grad):
    step = pl.program_id(0)

    @pl.when(step == 0)
    def _():
        for w in range(6):
            rows = pl.ds(w * 128, 128)
            values = x[rows].astype(F32) + dot(mixture[rows], out_weight[...])
            values = values.astype(BF16).astype(F32)
            quarters = [values[32 * j:32 * j + 32] for j in range(4)]
            center = sum(jnp.sum(part, axis=-1, keepdims=True) for part in quarters) * (1 / 4096)
            quarters = [part - center for part in quarters]
            spread = sum(jnp.sum(jnp.square(part), axis=-1, keepdims=True) for part in quarters) * (1 / 4096)
            inverse = lax.rsqrt(spread + epsilon)
            for j in range(4):
                normed[j, pl.ds(w * 32, 32)] = quarters[j] * inverse
            total[1, pl.ds(w * 32, 32)] = jnp.broadcast_to(inverse, (32, 1024))
        total[0] = jnp.zeros((192, 1024), F32)

    total[0] += dot(normed[step].astype(BF16), merge_weight[...])
    normed_grad[step] = dot(merged_grad[...], merge_weight[...], NT).astype(BF16).astype(F32)

    @pl.when(step == 3)
    def _():
        merged_out[...] = total[0].astype(BF16)
        for w in range(6):
            part = pl.ds(w * 32, 32)
            first = sum(jnp.sum(normed_grad[j, part], axis=-1, keepdims=True) for j in range(4)) * (1 / 4096)
            second = sum(jnp.sum(normed_grad[j, part] * normed[j, part], axis=-1, keepdims=True)
                         for j in range(4)) * (1 / 4096)
            inverse = total[1, part]
            for j in range(4):
                value = inverse * (normed_grad[j, part] - first - normed[j, part] * second)
                grad_out[pl.ds(w * 128 + j * 32, 32)] = value.astype(BF16)
        mixture_grad[...] = dot(grad_out[...], out_weight[...], NT).astype(BF16)


def merge_both(x, mixture, merged_grad, out_weight, merge_weight):
    whole = lambda rows: pl.BlockSpec((rows, 1024), lambda j: (0, 0))
    tokens = jax.ShapeDtypeStruct((768, 1024), BF16)
    return pl.pallas_call(
        merge_kernel,
        grid=(4,),
        out_shape=(jax.ShapeDtypeStruct((192, 1024), BF16), tokens, tokens),
        in_specs=[whole(768), whole(768), whole(192), whole(1024), pl.BlockSpec((1024, 1024), lambda j: (j, 0))],
        out_specs=(whole(192), whole(768), whole(768)),
        scratch_shapes=[pltpu.VMEM((4, 192, 1024), F32), pltpu.VMEM((2, 192, 1024), F32),
                        pltpu.VMEM((4, 192, 1024), F32)],
        compiler_params=params(), name="merge_both",
    )(x, mixture, merged_grad, out_weight, merge_weight)


def attend_back_kernel(q, k, v, p, mixture, mixture_grad, dq, dk, dv):
    masks = head_masks(128)
    row = lax.broadcasted_iota(jnp.int32, (512, 128), 0) // 128
    lane = lax.broadcasted_iota(jnp.int32, (512, 128), 1) // 32
    minus_heads = jnp.where(row == lane, -1.0, 0.0).astype(BF16)

    def own_heads(turned):
        return jnp.concatenate([turned[32 * head:32 * head + 32, 128 * head:128 * head + 128] for head in range(4)],
                               axis=0).T

    def column(wb, carry):
        for wa in range(2):
            w = wa * 3 + wb
            rows = pl.ds(pl.multiple_of(w * 128, 128), 128)
            for group in range(2):
                lanes = pl.ds(group * 128, 128)
                queries, keys, values = q[rows, lanes], k[rows, lanes], v[rows, lanes]
                out_grad = mixture_grad[rows, lanes]
                product = (out_grad.astype(F32) * mixture[rows, lanes].astype(F32)).astype(BF16)
                attention = p[w, group]
                change = dot(jnp.concatenate([out_grad, product], axis=1),
                             jnp.concatenate([spread_heads(values, masks), minus_heads], axis=1), NT)
                scores_grad = (attention.astype(F32) * change).astype(BF16)
                dq[rows, lanes] = (dot(scores_grad, spread_heads(keys, masks)) * SCALE).astype(BF16)
                dk[rows, lanes] = (own_heads(dot(queries, scores_grad, TN)) * SCALE).astype(BF16)
                dv[rows, lanes] = own_heads(dot(out_grad, attention, TN)).astype(BF16)
        return carry

    lax.fori_loop(0, 3, column, 0)


def attend_back(q, k, v, p, mixture, mixture_grad):
    tokens = jax.ShapeDtypeStruct((768, 1024), BF16)
    block = pl.BlockSpec((768, 256), lambda c: (0, c))
    return pl.pallas_call(
        attend_back_kernel,
        grid=(4,),
        out_shape=(tokens, tokens, tokens),
        in_specs=[block, block, block, pl.BlockSpec((6, 2, 128, 512), lambda c: (0, c, 0, 0)), block, block],
        out_specs=(block, block, block),
        compiler_params=params(), name="attend_back",
    )(q, k, v, p, mixture, mixture_grad)


MESH = pl.DeviceIdType.MESH
CHUNKS = 4
LANES = 512
WIDTH = 256


def place():
    lat, lon = lax.axis_index("lat"), lax.axis_index("lon")
    return (lat // 4) * 2 + (lon // 2) % 2, lon // 4, lat % 4, lon % 2


def device_at(x, y, z, core):
    return ((x // 2) * 4 + z, y * 4 + (x % 2) * 2 + core)


def finish_kernel(normed_turned, mix_turned, dq, dk, dv, grad, x_in, qkv_weight, order, qkv_out, out_out, framed_out,
                  g, normed_grad, from_core, acc_a, in_a, acc_b, in_b, acc_c, in_c, send, recv):
    x, y, z, core = place()
    here = (x, y, z)

    def moved(axis, step):
        there = list(here)
        there[axis] = (here[axis] + step) % 4
        return device_at(there[0], there[1], there[2], core)

    sibling = device_at(x, y, z, 1 - core)
    barrier = pltpu.get_barrier_semaphore()
    partners = [sibling] + [moved(axis, step) for axis in range(3) for step in (1, 2, 3)]
    for partner in partners:
        pl.semaphore_signal(barrier, inc=1, device_id=partner, device_id_type=MESH)
    pl.semaphore_wait(barrier, len(partners))

    started = []

    def push(stream, slot, source, target, partner):
        copy = pltpu.make_async_remote_copy(
            src_ref=source, dst_ref=target, send_sem=send.at[stream, slot],
            recv_sem=recv.at[stream, slot], device_id=partner, device_id_type=MESH)
        copy.start()
        started.append(copy)
        return copy

    def run(stream):
        chunk, part = stream // 2, stream % 2
        lanes = pl.ds(part * WIDTH, WIDTH)
        order = [(stream + k) % 3 for k in range(3)]
        mine = [here[axis] for axis in order]
        copy = push(stream, 0, g.at[chunk, :, 1 - core, :, lanes], from_core.at[stream], sibling)
        yield
        copy.wait_recv()

        def add_block(index, carry):
            a, b = index // 4, index % 4
            for c in range(4):
                at = [None, None, None]
                for axis, value in zip(order, (a, b, c)):
                    at[axis] = value
                row = ((at[0] // 2) * 4 + at[2]) * 8 + at[1] * 2 + at[0] % 2
                total = g[chunk, row, core, :, lanes].astype(F32) + from_core[stream, row].astype(F32)
                acc_a[stream, a, b * 4 + c] = total.astype(BF16)
            return carry

        lax.fori_loop(0, 16, add_block, 0)
        for level, (acc, arrived, blocks) in enumerate(((acc_a, in_a, 16), (acc_b, in_b, 4))):
            axis, p = order[level], mine[level]
            half = blocks // 2
            low, high = pl.ds(0, half), pl.ds(half, half)
            base = 1 + level * 6
            right, left = moved(axis, 1), moved(axis, 3)
            after, before, across = (p + 1) % 4, (p + 3) % 4, (p + 2) % 4
            relay_up = push(stream, base, acc.at[stream, across, high], arrived.at[stream, 0], right)
            relay_down = push(stream, base + 1, acc.at[stream, across, low], arrived.at[stream, 1], left)
            own_up = push(stream, base + 2, acc.at[stream, after, low], arrived.at[stream, 2], right)
            own_down = push(stream, base + 3, acc.at[stream, before, high], arrived.at[stream, 3], left)
            yield
            relay_up.wait_recv()
            acc[stream, after, high] = (acc[stream, after, high].astype(F32)
                                        + arrived[stream, 0].astype(F32)).astype(BF16)
            sum_up = push(stream, base + 4, acc.at[stream, after, high], arrived.at[stream, 4], right)
            relay_down.wait_recv()
            acc[stream, before, low] = (acc[stream, before, low].astype(F32)
                                        + arrived[stream, 1].astype(F32)).astype(BF16)
            sum_down = push(stream, base + 5, acc.at[stream, before, low], arrived.at[stream, 5], left)
            yield
            own_up.wait_recv()
            own_down.wait_recv()
            sum_up.wait_recv()
            sum_down.wait_recv()
            total_low = (acc[stream, p, low].astype(F32) + arrived[stream, 2].astype(F32)
                         + arrived[stream, 5].astype(F32)).astype(BF16)
            total_high = (acc[stream, p, high].astype(F32) + arrived[stream, 3].astype(F32)
                          + arrived[stream, 4].astype(F32)).astype(BF16)
            if level == 0:
                for i in range(2):
                    acc_b[stream, i] = total_low[i * 4:i * 4 + 4]
                    acc_b[stream, i + 2] = total_high[i * 4:i * 4 + 4]
            else:
                for i in range(2):
                    acc_c[stream, i] = total_low[i]
                    acc_c[stream, i + 2] = total_high[i]
        axis, p = order[2], mine[2]
        last = [push(stream, 13 + k, acc_c.at[stream, (p + k + 1) % 4], in_c.at[stream, k], moved(axis, k + 1))
                for k in range(3)]
        yield
        total = acc_c[stream, p].astype(F32)
        for k in range(3):
            last[k].wait_recv()
            total = total + in_c[stream, k].astype(F32)
        columns = WIDTH * chunk
        if part == 0:
            qkv_out[:, columns:columns + WIDTH] = total[:8]
            qkv_out[:, 2048 + columns:2048 + columns + WIDTH] = total[8:]
        else:
            qkv_out[:, 1024 + columns:1024 + columns + WIDTH] = total[:8]
            out_out[:, columns:columns + WIDTH] = total[8:]

    running = []

    def advance():
        for job in list(running):
            try:
                next(job)
            except StopIteration:
                running.remove(job)

    for chunk in range(CHUNKS):
        columns = slice(chunk * 256, chunk * 256 + 256)

        def weight_rows(i, carry):
            rows = pl.ds(pl.multiple_of(i * 256, 256), 256)
            pairs = pl.ds(i * 16, 16)
            normed_part = normed_turned[rows]
            for part, (upper, lower) in enumerate((
                    (dot(normed_part, dq[:, columns]), dot(normed_part, dv[:, columns])),
                    (dot(normed_part, dk[:, columns]), dot(mix_turned[rows], grad[:, columns])))):
                both = jnp.concatenate([upper.reshape(32, 8, 256), lower.reshape(32, 8, 256)], axis=1)
                g[chunk, pairs, :, :, part * WIDTH:part * WIDTH + WIDTH] = both.astype(BF16).reshape(16, 2, 16, 256)
            return carry

        lax.fori_loop(0, 4, weight_rows, 0)
        running.append(run(2 * chunk))
        running.append(run(2 * chunk + 1))
        advance()
    for i in range(4):
        rows = slice(i * 256, i * 256 + 256)
        normed_grad[:, rows] = (dot(dq[...], qkv_weight[rows, 0:1024], NT) + dot(dk[...], qkv_weight[rows, 1024:2048], NT)
                                + dot(dv[...], qkv_weight[rows, 2048:3072], NT))
        advance()

    def window(w, carry):
        rows = pl.ds(pl.multiple_of(w * 128, 128), 128)
        change = normed_grad[rows].astype(BF16).astype(F32)
        centered, inverse = statistics(x_in[rows].astype(F32))
        normed = centered * inverse
        first = jnp.mean(change, axis=-1, keepdims=True)
        second = jnp.mean(change * normed, axis=-1, keepdims=True)
        value = (inverse * (change - first - normed * second)).astype(BF16).astype(F32) + grad[rows].astype(F32)
        natural = dot(order[...], value.astype(BF16), TN)
        framed_out[w] = natural.reshape(2, 8, 8, 1024).astype(BF16)
        return carry

    for i in range(3):
        lax.fori_loop(2 * i, 2 * i + 2, window, 0)
        advance()
    while running:
        advance()
    for copy in started:
        copy.wait_send()


def finish(normed_turned, mix_turned, dq, dk, dv, grad, x, qkv_weight, order):
    streams = 2 * CHUNKS
    vmem = pl.BlockSpec(memory_space=pltpu.VMEM)
    return pl.pallas_call(
        finish_kernel,
        out_shape=(jax.ShapeDtypeStruct((8, 3072), F32), jax.ShapeDtypeStruct((8, 1024), F32),
                   jax.ShapeDtypeStruct((6, 2, 8, 8, 1024), BF16)),
        in_specs=[vmem] * 9,
        out_specs=(vmem, vmem, vmem),
        scratch_shapes=[
            pltpu.VMEM((CHUNKS, 64, 2, 16, LANES), BF16),
            pltpu.VMEM((768, 1024), F32),
            pltpu.VMEM((streams, 64, 16, WIDTH), BF16),
            pltpu.VMEM((streams, 4, 16, 16, WIDTH), BF16),
            pltpu.VMEM((streams, 6, 8, 16, WIDTH), BF16),
            pltpu.VMEM((streams, 4, 4, 16, WIDTH), BF16),
            pltpu.VMEM((streams, 6, 2, 16, WIDTH), BF16),
            pltpu.VMEM((streams, 4, 16, WIDTH), BF16),
            pltpu.VMEM((streams, 3, 16, WIDTH), BF16),
            pltpu.SemaphoreType.DMA((streams, 16)),
            pltpu.SemaphoreType.DMA((streams, 16)),
        ],
        compiler_params=pltpu.CompilerParams(collective_id=0, has_side_effects=True, vmem_limit_bytes=62 * MIB),
        name="finish",
    )(normed_turned, mix_turned, dq, dk, dv, grad, x, qkv_weight, order)


def shifted(block, axis, distance):
    devices = range(lax.axis_size(axis))
    route = [((i - distance) % len(devices), i) for i in devices]
    return lax.ppermute(block, axis, route)


def move_strips(grid_field, strip_width, offset):
    if offset == 1:
        outgoing = grid_field[:, :, -strip_width:]
    else:
        outgoing = grid_field[:, :, :strip_width]
    arrived = shifted(outgoing, "lon", offset)
    if offset == 1:
        middle = jnp.concatenate([arrived, grid_field[:, :, :-strip_width]], axis=2)
        outgoing_rows = middle[:, -strip_width:]
    else:
        middle = jnp.concatenate([grid_field[:, :, strip_width:], arrived], axis=2)
        outgoing_rows = middle[:, :strip_width]
    arrived_rows = shifted(outgoing_rows, "lat", offset)
    if offset == 1:
        return jnp.concatenate([arrived_rows, middle[:, :-strip_width]], axis=1)
    return jnp.concatenate([middle[:, strip_width:], arrived_rows], axis=1)


def to_groups(grid_field):
    return grid_field.reshape(2, 2, 4, 3, 4, 1024).transpose(1, 3, 0, 2, 4, 5).reshape(192, 1024)


def from_groups(groups):
    return groups.reshape(2, 3, 2, 4, 4, 1024).transpose(2, 0, 3, 1, 4, 5).reshape(2, 8, 12, 1024)


def shards(tokens, qkv_weight, out_weight, merge_weight, merged_grad):
    framed = move_strips(tokens, SHIFT, 1)
    framed_merged_grad = move_strips(merged_grad, SHIFT // 2, 1)
    order = jnp.asarray(window_order(), BF16)
    x, normed, normed_turned = prepare(framed, order)
    q, k, v, p, mixture, mix_turned = attend(normed, qkv_weight)
    merged_groups, grad, mixture_grad = merge_both(x, mixture, to_groups(framed_merged_grad), out_weight, merge_weight)
    merged = move_strips(from_groups(merged_groups), SHIFT // 2, -1)
    dq, dk, dv = attend_back(q, k, v, p, mixture, mixture_grad)
    qkv_weight_grad, out_weight_grad, framed_grad = finish(
        normed_turned, mix_turned, dq, dk, dv, grad, x, qkv_weight, order)
    framed_grad = framed_grad.reshape(2, 3, 2, 8, 8, 1024).transpose(2, 0, 3, 1, 4, 5).reshape(2, 16, 24, 1024)
    tokens_grad = move_strips(framed_grad, SHIFT, -1)
    return (merged, tokens_grad, qkv_weight_grad, out_weight_grad)


def solution(mesh):
    in_specs = (P(None, "lat", "lon", None), P(), P(), P(), P(None, "lat", "lon", None))
    out_specs = (
        P(None, "lat", "lon", None),
        P(None, "lat", "lon", None),
        P(("lat", "lon"), None),
        P(("lat", "lon"), None),
    )
    return jax.shard_map(shards, mesh=mesh, in_specs=in_specs, out_specs=out_specs, check_vma=False)
```

time: 437 us -> 176 us (0.40); the launches traced: 432 us -> 176 us
  local copies, waits for them, and re-layouts: 200 us -> 7.55 us
  matrix products: 105 us -> 0 us
  Pallas kernels: 36.3 us -> 121 us
  other arithmetic: 53.9 us -> 5.75 us
  waiting for transfers between devices: 17 us -> 25.2 us
    dot_general x14 -> x0, matrix products: 105 us -> none  [the longest x3 26.7 us: window_attention(): jnp.einsum('bqhd,bkhd->bhqk', queries, keys_part, preferred_element_type=...]
    pallas_call x1 -> x5, Pallas kernels: 36.3 us -> 121 us  [the longest x1 53 us: finish(): pl.pallas_call(finish_kernel, out_shape=(jax.ShapeDtypeStruct((8, 3072),...]
    reshape x7 -> x5, local copies, waits for them, and re-layouts: 65.9 us -> 1.53 us  [the longest x3 1.29 us: to_groups(): grid_field.reshape(2, 2, 4, 3, 4, 1024).transpose(1, 3, 0, 2, 4, 5)]
    convert_element_type x6 -> x0, local copies, waits for them, and re-layouts: 39.1 us -> none  [the longest x3 15.6 us: normalize(): values = grid_field.astype(jnp.float32)]
    unnamed x56 -> x12, local copies, waits for them, and re-layouts: 31.7 us -> 1.28 us
    add_any x1 -> x0, local copies, waits for them, and re-layouts: 25.8 us -> none  [window_attention(): queries = pieces[:, :, 0]]
    reduce_sum x6 -> x0, other arithmetic: 19.3 us -> none  [the longest x1 6.04 us: normalize(): (values - center) * lax.rsqrt(spread + epsilon)]
    slice x1 -> x0, local copies, waits for them, and re-layouts: 14.3 us -> none  [window_attention(): values_part = pieces[:, :, 2]]
  transfers between devices with their start and end apart: 8 -> 8, of which waited for: 3 -> 4; matrix products, arithmetic and copies ran while one was open for 12% -> 4% of each run, Pallas kernels for 8% -> 0%
where the time goes in v2:
time: 176 us
  Pallas kernels  121 us (69%)
  waiting for transfers between devices  25.2 us (14%)
  starting transfers between devices  15.6 us (9%)
  local copies, waits for them, and re-layouts  7.55 us (4%)
  other arithmetic  5.75 us (3%)
    pallas_call x1, Pallas kernels, finish(): pl.pallas_call(finish_kernel, out_shape=(jax.ShapeDtypeStruct((8, 3072),...  53 us
    pallas_call x1, Pallas kernels, attend(): pl.pallas_call(attend_kernel, grid=(4,), out_shape=(tokens, tokens, token...  25.8 us
    ppermute x8, waiting for transfers between devices, shifted(): return lax.ppermute(block, axis, route)  25.2 us
    pallas_call x1, Pallas kernels, attend_back(): pl.pallas_call(attend_back_kernel, grid=(4,), out_shape=(tokens, tokens,...  20.1 us
    pallas_call x1, Pallas kernels, merge_both(): pl.pallas_call(merge_kernel, grid=(4,), out_shape=(jax.ShapeDtypeStruct((...  16 us
    ppermute x8, starting transfers between devices, shifted(): return lax.ppermute(block, axis, route)  15.6 us
    pallas_call x1, Pallas kernels, prepare(): pl.pallas_call(prepare_kernel, grid=(6,), out_shape=(jax.ShapeDtypeStruct...  6.1 us
  transfers between devices with their start and end apart: 8, of which 4 were waited for; matrix products, arithmetic and copies ran while one was open for 4% of the time, Pallas kernels for 0%

profile of v2, /device:TPU:1, one launch (start us, length us, event | category | flops | bytes accessed | tf_op | source)
XLA Modules:
  0.0 175.9 jit_solution(8020949583351551782)
XLA Ops:
  0.6 1.2 slice.48
  1.9 2.7 %collective-permute-start = (bf16[2,16,4,1024]{3,2,1,0:T(4,128)(2,1)S(1)}, bf16[2,16,4,1024]{3,2,1,0:T(4,128)(2,1)S(1)}, u32[]{:S(2)}, u32[]{:S(2)}) collective-permute-start(bf16[2,16,4,1024]{3,2,1,0:T(4,128)(2,1)S(1)} %slice.48), channel_id=1, source_target_pairs={{15,0},{0,1},{1,2},{2,3},{3,4},{4,5},{5,6},{6,7},{7,8},{8,9},{9,10... | collective-permute-start | bytes 786440 | tf_op jit(solution)/shard_map/ppermute | solution.py:424
  4.5 0.8 slice.52
  5.4 2.5 %collective-permute-done = bf16[2,16,4,1024]{3,2,1,0:T(4,128)(2,1)S(1)} collective-permute-done((bf16[2,16,4,1024]{3,2,1,0:T(4,128)(2,1)S(1)}, bf16[2,16,4,1024]{3,2,1,0:T(4,128)(2,1)S(1)}, u32[]{:S(2)}, u32[]{:S(2)}) %collective-permute-start) | collective-permute-done | bytes 262176 | tf_op jit(solution)/shard_map/ppermute | solution.py:424
  7.9 1.1 pad_maximum_fusion.4
  9.0 1.7 collective-permute-start.1
  10.9 1.7 collective-permute-start.3
  12.6 10.2 %collective-permute-done.3 = bf16[2,2,12,1024]{3,1,2,0:T(2,128)(2,1)S(1)} collective-permute-done((bf16[2,2,12,1024]{3,1,2,0:T(2,128)(2,1)S(1)}, bf16[2,2,12,1024]{3,1,2,0:T(2,128)(2,1)S(1)}, u32[]{:S(2)}, u32[]{:S(2)}) %collective-permute-start.3) | collective-permute-done | bytes 98336 | tf_op jit(solution)/shard_map/ppermute | solution.py:424
  22.7 0.2 fusion.2
  22.9 0.1 reshape.26
  23.1 0.3 copy.14
  23.4 0.8 reshape.27.merged_grad
  24.2 1.7 fusion.framed
  25.9 6.1 %prepare.1 = (bf16[768,1024]{1,0:T(8,128)(2,1)}, bf16[768,1024]{1,0:T(8,128)(2,1)}, bf16[1024,768]{1,0:T(8,128)(2,1)}) custom-call(bf16[2,16,24,1024]{3,2,1,0:T(8,128)(2,1)} %fusion.framed, bf16[128,128]{1,0:T(8,128)(2,1)} %constant.2.clone.order), custom_call_target="tpu_custom_call" | custom-call | tf_op jit(solution)/shard_map/prepare/pallas_call | solution.py:51
  32.0 25.8 %attend.1 = (bf16[768,1024]{1,0:T(8,128)(2,1)}, bf16[768,1024]{1,0:T(8,128)(2,1)}, bf16[768,1024]{1,0:T(8,128)(2,1)}, bf16[6,8,128,512]{3,2,1,0:T(8,128)(2,1)}, ...) custom-call(bf16[768,1024]{1,0:T(8,128)(2,1)} %get-tuple-element.23.normed, bf16[1024,3072]{1,0:T(8,128)(2,1)} %qkv_weight.1, ...), custom_call_target="tpu_custom_call" | custom-call | tf_op jit(solution)/shard_map/attend/pallas_call | solution.py:115
  57.8 16.0 %merge_both.1 = (bf16[192,1024]{1,0:T(8,128)(2,1)}, bf16[768,1024]{1,0:T(8,128)(2,1)}, bf16[768,1024]{1,0:T(8,128)(2,1)}) custom-call(bf16[768,1024]{1,0:T(8,128)(2,1)} %get-tuple-element.22.x.x_in, bf16[768,1024]{1,0:T(8,128)(2,1)} %get-tuple-element.24.mixture, bf16[192,1024]{1,0:T(8,128)(2,1)} %reshape.27.merged_grad, bf16[1024,1024]{1,0:T(8,128)(2,1)} %out_weight.1, ...), custom_call_target="tpu_custom_call" | custom-call | tf_op jit(solution)/shard_map/merge_both/pallas_call | solution.py:168
  73.9 20.1 %attend_back.1 = (bf16[768,1024]{1,0:T(8,128)(2,1)}, bf16[768,1024]{1,0:T(8,128)(2,1)}, bf16[768,1024]{1,0:T(8,128)(2,1)}) custom-call(bf16[768,1024]{1,0:T(8,128)(2,1)} %get-tuple-element.28.q, bf16[768,1024]{1,0:T(8,128)(2,1)} %get-tuple-element.29.k, bf16[768,1024]{1,0:T(8,128)(2,1)} %get-tuple-element.30.v, ...), custom_call_target="tpu_custom_call" | custom-call | tf_op jit(solution)/shard_map/attend_back/pallas_call | solution.py:214
  94.0 53.0 %finish.1 = (f32[8,3072]{1,0:T(8,128)}, f32[8,1024]{1,0:T(8,128)}, bf16[6,2,8,8,1024]{4,3,2,1,0:T(8,128)(2,1)}) custom-call(bf16[1024,768]{1,0:T(8,128)(2,1)} %get-tuple-element.26.normed_turned, bf16[1024,768]{1,0:T(8,128)(2,1)} %get-tuple-element.27.mix_turned, bf16[768,1024]{1,0:T(8,128)(2,1)} %get-tuple-element.33.dq, ...), custom_call_target="tpu_custom_call" | custom-call | tf_op jit(solution)/shard_map/finish/pallas_call | solution.py:397
  147.0 1.6 copy.12
  148.7 5.0 %collective-permute-start.6 = (bf16[2,16,4,1024]{3,2,1,0:T(4,128)(2,1)S(1)}, bf16[2,16,4,1024]{3,2,1,0:T(4,128)(2,1)S(1)}, u32[]{:S(2)}, u32[]{:S(2)}) collective-permute-start(bf16[2,16,4,1024]{3,2,1,0:T(4,128)(2,1)S(1)} %slice.69), channel_id=1, source_target_pairs={{1,0},{2,1},{3,2},{4,3},{5,4},{6,5},{7,6},{8,7},{9,8},{10,9},{11,1... | collective-permute-start | bytes 786440 | tf_op jit(solution)/shard_map/ppermute | solution.py:424
  153.7 0.1 reshape.28
  153.8 0.2 copy.11
  154.2 0.7 slice.68
  155.0 2.8 %collective-permute-done.6 = bf16[2,16,4,1024]{3,2,1,0:T(4,128)(2,1)S(1)} collective-permute-done((bf16[2,16,4,1024]{3,2,1,0:T(4,128)(2,1)S(1)}, bf16[2,16,4,1024]{3,2,1,0:T(4,128)(2,1)S(1)}, u32[]{:S(2)}, u32[]{:S(2)}) %collective-permute-start.6) | collective-permute-done | bytes 262176 | tf_op jit(solution)/shard_map/ppermute | solution.py:424
  157.9 3.7 %collective-permute-start.7 = (bf16[2,4,24,1024]{3,2,1,0:T(8,128)(2,1)S(1)}, bf16[2,4,24,1024]{3,2,1,0:T(8,128)(2,1)S(1)}, u32[]{:S(2)}, u32[]{:S(2)}) collective-permute-start(bf16[2,4,24,1024]{3,2,1,0:T(8,128)(2,1)S(1)} %pad_maximum_fusion.2), channel_id=1, source_target_pairs={{16,0},{32,16},{48,32},{64,48},{80,64},{96,80},{112,96},{0,112},{1... | collective-permute-start | bytes 1179656 | tf_op jit(solution)/shard_map/ppermute | solution.py:424
  161.7 0.6 collective-permute-start.5
  162.4 9.8 %collective-permute-done.5 = bf16[2,2,12,1024]{3,1,2,0:T(2,128)(2,1)S(1)} collective-permute-done((bf16[2,2,12,1024]{3,1,2,0:T(2,128)(2,1)S(1)}, bf16[2,2,12,1024]{3,1,2,0:T(2,128)(2,1)S(1)}, u32[]{:S(2)}, u32[]{:S(2)}) %collective-permute-start.5) | collective-permute-done | bytes 98336 | tf_op jit(solution)/shard_map/ppermute | solution.py:424
  172.2 0.9 pad_maximum_fusion.5
  173.1 0.2 fusion.1
  173.4 1.3 pad_maximum_fusion.1
  174.7 0.6 copy.17
  175.3 0.6 copy.18
  (25 shorter events, 0.7 us)
Async XLA Ops:
  0.6 10.1 %copy-start.1 = (bf16[2,8,12,1024]{3,1,2,0:T(8,128)(2,1)S(1)}, bf16[2,8,12,1024]{3,1,2,0:T(8,128)(2,1)}, u32[]{:S(2)}) copy-start(bf16[2,8,12,1024]{3,1,2,0:T(8,128)(2,1)} %param.10) | copy-start | bytes 1179652
  1.9 6.0 %collective-permute-start = (bf16[2,16,4,1024]{3,2,1,0:T(4,128)(2,1)S(1)}, bf16[2,16,4,1024]{3,2,1,0:T(4,128)(2,1)S(1)}, u32[]{:S(2)}, u32[]{:S(2)}) collective-permute-start(bf16[2,16,4,1024]{3,2,1,0:T(4,128)(2,1)S(1)} %slice.48), channel_id=1, source_target_pairs={{15,0},{0,1},{1,2},{2,3},{3,4},{4,5},{5,6},{6,7},{7,8},{8,9},{9,10... | collective-permute-start | bytes 786440 | tf_op jit(solution)/shard_map/ppermute | solution.py:424
  5.4 5.3 %collective-permute-start.2 = (bf16[2,8,2,1024]{3,1,2,0:T(8,128)(2,1)S(1)}, bf16[2,8,2,1024]{3,1,2,0:T(8,128)(2,1)S(1)}, u32[]{:S(2)}, u32[]{:S(2)}) collective-permute-start(bf16[2,8,2,1024]{3,1,2,0:T(8,128)(2,1)S(1)} %slice.52), channel_id=1, source_target_pairs={{15,0},{0,1},{1,2},{2,3},{3,4},{4,5},{5,6},{6,7},{7,8},{8,9},{9,10... | collective-permute-start | bytes 196616 | tf_op jit(solution)/shard_map/ppermute | solution.py:424
  9.0 15.2 %collective-permute-start.1 = (bf16[2,4,24,1024]{3,2,1,0:T(8,128)(2,1)S(1)}, bf16[2,4,24,1024]{3,2,1,0:T(8,128)(2,1)S(1)}, u32[]{:S(2)}, u32[]{:S(2)}) collective-permute-start(bf16[2,4,24,1024]{3,2,1,0:T(8,128)(2,1)S(1)} %pad_maximum_fusion.4), channel_id=1, source_target_pairs={{112,0},{0,16},{16,32},{32,48},{48,64},{64,80},{80,96},{96,112},{1... | collective-permute-start | bytes 1179656 | tf_op jit(solution)/shard_map/ppermute | solution.py:424
  10.9 13.4 %copy-start = (bf16[2,16,24,1024]{3,2,1,0:T(8,128)(2,1)S(1)}, bf16[2,16,24,1024]{3,2,1,0:T(8,128)(2,1)}, u32[]{:S(2)}) copy-start(bf16[2,16,24,1024]{3,2,1,0:T(8,128)(2,1)} %param.6) | copy-start | bytes 4718596
  10.9 11.9 %collective-permute-start.3 = (bf16[2,2,12,1024]{3,1,2,0:T(2,128)(2,1)S(1)}, bf16[2,2,12,1024]{3,1,2,0:T(2,128)(2,1)S(1)}, u32[]{:S(2)}, u32[]{:S(2)}) collective-permute-start(bf16[2,2,12,1024]{3,1,2,0:T(2,128)(2,1)S(1)} %pad_maximum_fusion.7), channel_id=1, source_target_pairs={{112,0},{0,16},{16,32},{32,48},{48,64},{64,80},{80,96},{96,112},{1... | collective-permute-start | bytes 294920 | tf_op jit(solution)/shard_map/ppermute | solution.py:424
  147.0 6.7 %copy-start.2 = (bf16[192,1024]{1,0:T(8,128)(2,1)S(1)}, bf16[192,1024]{1,0:T(8,128)(2,1)}, u32[]{:S(2)}) copy-start(bf16[192,1024]{1,0:T(8,128)(2,1)} %get-tuple-element.25) | copy-start | bytes 1179652
  148.7 9.1 %collective-permute-start.6 = (bf16[2,16,4,1024]{3,2,1,0:T(4,128)(2,1)S(1)}, bf16[2,16,4,1024]{3,2,1,0:T(4,128)(2,1)S(1)}, u32[]{:S(2)}, u32[]{:S(2)}) collective-permute-start(bf16[2,16,4,1024]{3,2,1,0:T(4,128)(2,1)S(1)} %slice.69), channel_id=1, source_target_pairs={{1,0},{2,1},{3,2},{4,3},{5,4},{6,5},{7,6},{8,7},{9,8},{10,9},{11,1... | collective-permute-start | bytes 786440 | tf_op jit(solution)/shard_map/ppermute | solution.py:424
  154.9 6.7 %collective-permute-start.4 = (bf16[2,8,2,1024]{3,1,2,0:T(8,128)(2,1)S(1)}, bf16[2,8,2,1024]{3,1,2,0:T(8,128)(2,1)S(1)}, u32[]{:S(2)}, u32[]{:S(2)}) collective-permute-start(bf16[2,8,2,1024]{3,1,2,0:T(8,128)(2,1)S(1)} %slice.65), channel_id=1, source_target_pairs={{1,0},{2,1},{3,2},{4,3},{5,4},{6,5},{7,6},{8,7},{9,8},{10,9},{11,1... | collective-permute-start | bytes 196616 | tf_op jit(solution)/shard_map/ppermute | solution.py:424
  157.9 15.5 %collective-permute-start.7 = (bf16[2,4,24,1024]{3,2,1,0:T(8,128)(2,1)S(1)}, bf16[2,4,24,1024]{3,2,1,0:T(8,128)(2,1)S(1)}, u32[]{:S(2)}, u32[]{:S(2)}) collective-permute-start(bf16[2,4,24,1024]{3,2,1,0:T(8,128)(2,1)S(1)} %pad_maximum_fusion.2), channel_id=1, source_target_pairs={{16,0},{32,16},{48,32},{64,48},{80,64},{96,80},{112,96},{0,112},{1... | collective-permute-start | bytes 1179656 | tf_op jit(solution)/shard_map/ppermute | solution.py:424
  161.7 10.5 %collective-permute-start.5 = (bf16[2,2,12,1024]{3,1,2,0:T(2,128)(2,1)S(1)}, bf16[2,2,12,1024]{3,1,2,0:T(2,128)(2,1)S(1)}, u32[]{:S(2)}, u32[]{:S(2)}) collective-permute-start(bf16[2,2,12,1024]{3,1,2,0:T(2,128)(2,1)S(1)} %pad_maximum_fusion.6), channel_id=1, source_target_pairs={{16,0},{32,16},{48,32},{64,48},{80,64},{96,80},{112,96},{0,112},{1... | collective-permute-start | bytes 294920 | tf_op jit(solution)/shard_map/ppermute | solution.py:424
  173.4 1.3 copy-start.3
  173.4 1.9 %copy-start.4 = (f32[8,1024]{1,0:T(8,128)S(1)}, f32[8,1024]{1,0:T(8,128)}, u32[]{:S(2)}) copy-start(f32[8,1024]{1,0:T(8,128)} %get-tuple-element.47) | copy-start | bytes 98308

commit v3 on v0

v3 whole, which is shorter than its diff:
```python
import jax
import jax.numpy as jnp
import numpy as np
from jax import lax
from jax.experimental import pallas as pl
from jax.experimental.pallas import tpu as pltpu
from jax.sharding import PartitionSpec as P

SHIFT = 4
CHUNKS = 4
LANES = 512
WIDTH = 256
MESH = pl.DeviceIdType.MESH
F32, BF16 = jnp.float32, jnp.bfloat16
epsilon = 1e-05
SCALE = 32 ** -0.5
MIB = 1024 * 1024
NT = (((1,), (1,)), ((), ()))
TN = (((0,), (0,)), ((), ()))


def params(limit=60):
    return pltpu.CompilerParams(vmem_limit_bytes=limit * MIB)


def dot(left, right, dims=(((1,), (0,)), ((), ()))):
    return lax.dot_general(left, right, dims, preferred_element_type=F32)


def picks(index):
    return (index[:, None] == np.arange(len(index))[None, :]).astype(np.float32)


def window_order():
    t = np.arange(128)
    quarter, level, a, b = t // 32, t // 16 % 2, t // 4 % 4, t % 4
    return picks((level * 8 + 2 * a + quarter % 2) * 8 + 2 * b + quarter // 2)


def orders():
    n = np.arange(128)
    level, i, j = n // 64, n // 8 % 8, n % 8
    to_natural = picks((((i // 4) * 2 + j // 4) * 2 + level) * 16 + (i % 4) * 4 + j % 4)
    to_quarters = window_order() @ to_natural
    n = np.arange(192)
    level, i, j = n // 96, n // 12 % 8, n % 12
    merged_natural = picks((((i // 2) * 6 + j // 2) * 2 + level) * 4 + (i % 2) * 2 + j % 2)
    window, level, a, b = n // 32, n // 16 % 2, n // 4 % 4, n % 4
    row, column = 2 * (window // 3) + a // 2, 2 * (window % 3) + b // 2
    merged_windows = picks(((row * 6 + column) * 2 + level) * 4 + (a % 2) * 2 + b % 2)
    return tuple(jnp.asarray(order, BF16) for order in (to_natural, to_quarters, merged_natural, merged_windows))


def statistics(values):
    center = jnp.mean(values, axis=-1, keepdims=True)
    shifted_values = values - center
    spread = jnp.mean(jnp.square(shifted_values), axis=-1, keepdims=True)
    return shifted_values, lax.rsqrt(spread + epsilon)


def prepare_kernel(framed, order, x_out, normed_out, normed_turned):
    natural = framed[...].astype(F32).reshape(128, 1024).astype(BF16)
    values = dot(order[...], natural)
    x_out[...] = values.astype(BF16)
    centered, inverse = statistics(values)
    normed = centered * inverse
    normed_out[...] = normed.astype(BF16)
    normed_turned[...] = normed.T.astype(BF16)


def prepare(framed, order):
    return pl.pallas_call(
        prepare_kernel,
        grid=(6,),
        out_shape=(jax.ShapeDtypeStruct((768, 1024), BF16), jax.ShapeDtypeStruct((768, 1024), BF16),
                   jax.ShapeDtypeStruct((1024, 768), BF16)),
        in_specs=[pl.BlockSpec((2, 8, 8, 1024), lambda w: (0, w // 3, w % 3, 0)),
                  pl.BlockSpec((128, 128), lambda w: (0, 0))],
        out_specs=(pl.BlockSpec((128, 1024), lambda w: (w, 0)), pl.BlockSpec((128, 1024), lambda w: (w, 0)),
                   pl.BlockSpec((1024, 128), lambda w: (0, w))),
        compiler_params=params(), name="prepare",
    )(framed, order)


def place():
    lat, lon = lax.axis_index("lat"), lax.axis_index("lon")
    return (lat // 4) * 2 + (lon // 2) % 2, lon // 4, lat % 4, lon % 2


def device_at(x, y, z, core):
    return ((x // 2) * 4 + z, y * 4 + (x % 2) * 2 + core)


def neighbours(step):
    lat, lon = lax.axis_index("lat"), lax.axis_index("lon")
    lat_there, lon_there = (lat + step + 8) % 8, (lon + step + 16) % 16
    return (lat_there, lon), (lat, lon_there), (lat_there, lon_there)


def greet(receive_from, send_to):
    barrier = pltpu.get_barrier_semaphore()
    for device in receive_from:
        pl.semaphore_signal(barrier, inc=1, device_id=device, device_id_type=MESH)
    pl.semaphore_wait(barrier, len(send_to))


def remote(source, target, send, recv, device):
    return pltpu.make_async_remote_copy(src_ref=source, dst_ref=target, send_sem=send, recv_sem=recv,
                                        device_id=device, device_id_type=MESH)


def frame_copies(units, first, last, send, recv, base, devices):
    row, column, corner = devices
    return [remote(units.at[first[0], 1:6], units.at[last[0], 1:6], send.at[base], recv.at[base], row),
            remote(units.at[1:4, first[1]], units.at[1:4, last[1]], send.at[base + 1], recv.at[base + 1], column),
            remote(units.at[first[0], first[1]], units.at[last[0], last[1]], send.at[base + 2], recv.at[base + 2], corner)]


def wide_masks():
    lane = lax.broadcasted_iota(jnp.int32, (128, 256), 1)
    return [lane % 128 // 32 == head for head in range(4)], [lane // 128 == group for group in range(2)]


def stack(values, masks):
    zero = jnp.zeros_like(values)
    return jnp.concatenate([jnp.where(mask, values, zero) for mask in masks], axis=0)


def select(stacked, masks):
    rows = [stacked[128 * head:128 * head + 128] for head in range(4)]
    return jnp.where(masks[0], rows[0], jnp.where(masks[1], rows[1], jnp.where(masks[2], rows[2], rows[3])))


def other_region(rows, columns, edge):
    row = (lax.broadcasted_iota(jnp.int32, (rows, 1), 0) // 4 % 4 < 2) & edge
    column = (lax.broadcasted_iota(jnp.int32, (1, columns), 1) // 4 % 4 < 2) & edge
    return row.astype(jnp.int32) != column.astype(jnp.int32)


def back_kernel(q_hbm, k_hbm, v_hbm, mix_hbm, mix_grad_hbm, normed_hbm, mix_turned_hbm, grad_hbm, x_hbm, weight_hbm,
                merged_in, to_natural, to_quarters, merged_natural, merged_windows,
                qkv_out, out_out, tokens_out, merged_out,
                q, k, v, mix, mix_grad, normed_turned, mix_turned, grad, x_in, qkv_weight,
                dq, dk, dv, g, normed_grad, units, merged_units,
                from_core, acc_a, in_a, acc_b, in_b, acc_c, in_c, load, send, recv, strip_send, strip_recv):
    loads = {}

    def fetch(name, index, source, target):
        loads[name] = pltpu.make_async_copy(source, target, load.at[index])
        loads[name].start()

    wide = ((q_hbm, q), (k_hbm, k), (v_hbm, v), (mix_hbm, mix), (mix_grad_hbm, mix_grad))
    for chunk in range(CHUNKS):
        columns = pl.ds(chunk * 256, 256)
        for i, (source, target) in enumerate(wide):
            fetch((chunk, i), chunk * 5 + i, source.at[:, columns], target.at[:, columns])
        if chunk == 0:
            fetch("normed", 20, normed_hbm, normed_turned)
            fetch("mix", 21, mix_turned_hbm, mix_turned)
            fetch("grad", 22, grad_hbm, grad)
    fetch("weight", 23, weight_hbm, qkv_weight)
    fetch("x", 24, x_hbm, x_in)

    x, y, z, core = place()
    here = (x, y, z)

    def moved(axis, step):
        there = list(here)
        there[axis] = (here[axis] + step) % 4
        return device_at(there[0], there[1], there[2], core)

    sibling = device_at(x, y, z, 1 - core)
    ring = [sibling] + [moved(axis, step) for axis in range(3) for step in (1, 2, 3)]
    before, after = neighbours(-1), neighbours(1)
    greet(ring + list(after), ring + list(before))

    started = []

    def push(copy):
        copy.start()
        started.append(copy)
        return copy

    units_in = dot(merged_windows[...], merged_in[...], TN).reshape(4, 6, 8, 1024)
    for i in range(4):
        merged_units[i, 0:6] = units_in[i]
    merged_copies = frame_copies(merged_units, (0, 0), (4, 6), strip_send, strip_recv, 0, before)
    for copy in merged_copies:
        push(copy)

    def run(stream):
        chunk, part = stream // 2, stream % 2
        slot = chunk % 2
        lanes = pl.ds(part * WIDTH, WIDTH)
        order = [(stream + i) % 3 for i in range(3)]
        mine = [here[axis] for axis in order]
        copy = push(remote(g.at[slot, :, 1 - core, :, lanes], from_core.at[stream],
                           send.at[stream, 0], recv.at[stream, 0], sibling))
        yield
        copy.wait_recv()

        def add_block(index, carry):
            a, b = index // 4, index % 4
            for c in range(4):
                at = [None, None, None]
                for axis, value in zip(order, (a, b, c)):
                    at[axis] = value
                row = ((at[0] // 2) * 4 + at[2]) * 8 + at[1] * 2 + at[0] % 2
                total = g[slot, row, core, :, lanes].astype(F32) + from_core[stream, row].astype(F32)
                acc_a[stream, a, b * 4 + c] = total.astype(BF16)
            return carry

        lax.fori_loop(0, 16, add_block, 0)
        for level, (acc, arrived) in enumerate(((acc_a, in_a), (acc_b, in_b), (acc_c, in_c))):
            axis, p = order[level], mine[level]
            copies = [push(remote(acc.at[stream, (p + i + 1) % 4], arrived.at[stream, i],
                                  send.at[stream, 1 + level * 3 + i], recv.at[stream, 1 + level * 3 + i],
                                  moved(axis, i + 1))) for i in range(3)]
            yield
            for copy in copies:
                copy.wait_recv()
            total = acc[stream, p].astype(F32)
            for i in range(3):
                total = total + arrived[stream, i].astype(F32)
            if level == 0:
                for i in range(4):
                    acc_b[stream, i] = total[i * 4:i * 4 + 4].astype(BF16)
            elif level == 1:
                for i in range(4):
                    acc_c[stream, i] = total[i].astype(BF16)
        columns = WIDTH * chunk
        if part == 0:
            qkv_out[:, columns:columns + WIDTH] = total[:8]
            qkv_out[:, 2048 + columns:2048 + columns + WIDTH] = total[8:]
        else:
            qkv_out[:, 1024 + columns:1024 + columns + WIDTH] = total[:8]
            out_out[:, columns:columns + WIDTH] = total[8:]

    running = []

    def advance():
        for job in list(running):
            try:
                next(job)
            except StopIteration:
                running.remove(job)

    head_mask, group_mask = wide_masks()
    row8 = lax.broadcasted_iota(jnp.int32, (8, 256), 0)
    lane8 = lax.broadcasted_iota(jnp.int32, (8, 256), 1) // 32
    own_head = jnp.where(lane8 == row8, 1.0, 0.0).astype(BF16)
    edge = lax.axis_index("lat") == 0
    first_send = {}
    for chunk in range(CHUNKS):
        columns = slice(chunk * 256, chunk * 256 + 256)
        for i in range(5):
            loads[(chunk, i)].wait()

        def window_back(wa):
            for wb in range(3):
                rows = pl.ds(pl.multiple_of(wa * 384 + wb * 128, 128), 128)
                queries, keys, values = q[rows, columns], k[rows, columns], v[rows, columns]
                out_grad = mix_grad[rows, columns]
                product = (out_grad.astype(F32) * mix[rows, columns].astype(F32)).astype(BF16)
                spread_queries, spread_grads = stack(queries, group_mask), stack(out_grad, group_mask)
                weights = jnp.exp(dot(stack(keys, head_mask), spread_queries, NT) * SCALE)
                weights = jnp.where(other_region(512, 256, edge & (wa == 0)), 0.0, weights)
                change = dot(stack(values, head_mask), spread_grads, NT)
                means = dot(own_head, product, NT)
                attention, scores_grad = [], []
                for head in range(4):
                    part = weights[128 * head:128 * head + 128]
                    part = part * (1.0 / jnp.sum(part, axis=0, keepdims=True))
                    mean = jnp.concatenate([means[head:head + 1], means[4 + head:5 + head]], axis=1)
                    attention.append(part.astype(BF16))
                    scores_grad.append((part * (change[128 * head:128 * head + 128] - mean)).astype(BF16))
                dv[rows, columns] = select(dot(jnp.concatenate(attention, axis=0), spread_grads), head_mask).astype(BF16)
                dk[rows, columns] = (select(dot(jnp.concatenate(scores_grad, axis=0), spread_queries), head_mask)
                                     * SCALE).astype(BF16)
                turned = keys.T
                pieces = []
                for group in range(2):
                    for head in range(4):
                        low = group * 128 + head * 32
                        pieces.append(dot(turned[low:low + 32], scores_grad[head][:, group * 128:group * 128 + 128]))
                dq[rows, columns] = (jnp.concatenate(pieces, axis=0).T * SCALE).astype(BF16)

        pl.loop(0, 2)(window_back)
        if chunk == 0:
            for name in ("normed", "mix", "grad"):
                loads[name].wait()
        slot = chunk % 2
        if chunk >= 2:
            for copy in first_send[chunk - 2]:
                copy.wait_send()

        def weight_rows(i, carry):
            rows = pl.ds(pl.multiple_of(i * 256, 256), 256)
            pairs = pl.ds(i * 16, 16)
            normed_part = normed_turned[rows]
            for part, (upper, lower) in enumerate((
                    (dot(normed_part, dq[:, columns]), dot(normed_part, dv[:, columns])),
                    (dot(normed_part, dk[:, columns]), dot(mix_turned[rows], grad[:, columns])))):
                both = jnp.concatenate([upper.reshape(32, 8, 256), lower.reshape(32, 8, 256)], axis=1)
                g[slot, pairs, :, :, part * WIDTH:part * WIDTH + WIDTH] = both.astype(BF16).reshape(16, 2, 16, 256)
            return carry

        lax.fori_loop(0, 4, weight_rows, 0)
        advance()
        for part in range(2):
            job = run(2 * chunk + part)
            next(job)
            running.append(job)
        first_send[chunk] = started[-2:]
        del started[-2:]
    loads["weight"].wait()
    loads["x"].wait()

    def finish_window(w):
        rows = pl.ds(w * 128, 128)
        change = normed_grad[rows].astype(BF16).astype(F32)
        centered, inverse = statistics(x_in[rows].astype(F32))
        normed = centered * inverse
        first = jnp.mean(change, axis=-1, keepdims=True)
        second = jnp.mean(change * normed, axis=-1, keepdims=True)
        value = (inverse * (change - first - normed * second)).astype(BF16).astype(F32) + grad[rows].astype(F32)
        quarters = dot(to_quarters[...], value.astype(BF16), TN).astype(BF16).reshape(4, 32, 1024)
        wa, wb = w // 3, w % 3
        for u in range(2):
            for side in range(2):
                units[2 * wa + u, 2 * wb + side] = quarters[2 * u + side]

    strips = frame_copies(units, (0, 0), (4, 6), strip_send, strip_recv, 3, before)
    for half in range(2):
        tokens = slice(half * 384, half * 384 + 384)
        for i in range(4):
            rows = slice(i * 256, i * 256 + 256)
            normed_grad[tokens, rows] = (dot(dq[tokens], qkv_weight[rows, 0:1024], NT)
                                         + dot(dk[tokens], qkv_weight[rows, 1024:2048], NT)
                                         + dot(dv[tokens], qkv_weight[rows, 2048:3072], NT))
            if i % 2 == 1 and (half, i) != (1, 1):
                advance()
        for wb in range(3):
            finish_window(half * 3 + wb)
            if half == 1 and wb == 0:
                push(strips[1])
        if half == 0:
            push(strips[0])
            push(strips[2])
    for copy in merged_copies:
        copy.wait_recv()
    merged_natural_units = jnp.concatenate([merged_units[i, 1:7].reshape(48, 1024) for i in range(1, 5)], axis=0)
    merged_out[...] = dot(merged_natural[...], merged_natural_units.astype(BF16)).astype(BF16)
    advance()
    for copy in strips:
        copy.wait_recv()
    for m in range(2):
        blocks = []
        for n in range(3):
            parts = [units[2 * m + 1 + u, 2 * n + 1 + side] for u in range(2) for side in range(2)]
            natural = dot(to_natural[...], jnp.concatenate(parts, axis=0)).reshape(2, 8, 8, 1024)
            blocks.append(natural)
        tokens_out[:, 8 * m:8 * m + 8] = jnp.concatenate(blocks, axis=2).astype(BF16)
    while running:
        advance()
    for chunk in range(2, CHUNKS):
        for copy in first_send[chunk]:
            copy.wait_send()
    for copy in started:
        copy.wait_send()


def back(q, k, v, mix, mix_grad, normed_turned, mix_turned, grad, x, qkv_weight, merged_groups):
    streams = 2 * CHUNKS
    vmem, anywhere = pl.BlockSpec(memory_space=pltpu.VMEM), pl.BlockSpec(memory_space=pl.ANY)
    tokens = pltpu.VMEM((768, 1024), BF16)
    turned = pltpu.VMEM((1024, 768), BF16)
    return pl.pallas_call(
        back_kernel,
        out_shape=(jax.ShapeDtypeStruct((8, 3072), F32), jax.ShapeDtypeStruct((8, 1024), F32),
                   jax.ShapeDtypeStruct((2, 16, 24, 1024), BF16), jax.ShapeDtypeStruct((192, 1024), BF16)),
        in_specs=[anywhere] * 10 + [vmem] * 5,
        out_specs=(vmem, vmem, vmem, vmem),
        scratch_shapes=[
            tokens, tokens, tokens, tokens, tokens, turned, turned, tokens, tokens, pltpu.VMEM((1024, 3072), BF16),
            tokens, tokens, tokens,
            pltpu.VMEM((2, 64, 2, 16, LANES), BF16),
            pltpu.VMEM((768, 1024), F32),
            pltpu.VMEM((5, 7, 32, 1024), BF16),
            pltpu.VMEM((5, 7, 8, 1024), F32),
            pltpu.VMEM((streams, 64, 16, WIDTH), BF16),
            pltpu.VMEM((streams, 4, 16, 16, WIDTH), BF16),
            pltpu.VMEM((streams, 3, 16, 16, WIDTH), BF16),
            pltpu.VMEM((streams, 4, 4, 16, WIDTH), BF16),
            pltpu.VMEM((streams, 3, 4, 16, WIDTH), BF16),
            pltpu.VMEM((streams, 4, 16, WIDTH), BF16),
            pltpu.VMEM((streams, 3, 16, WIDTH), BF16),
            pltpu.SemaphoreType.DMA((25,)),
            pltpu.SemaphoreType.DMA((streams, 10)),
            pltpu.SemaphoreType.DMA((streams, 10)),
            pltpu.SemaphoreType.DMA((6,)),
            pltpu.SemaphoreType.DMA((6,)),
        ],
        compiler_params=pltpu.CompilerParams(collective_id=0, has_side_effects=True, vmem_limit_bytes=62 * MIB),
        name="back",
    )(q, k, v, mix, mix_grad, normed_turned, mix_turned, grad, x, qkv_weight, merged_groups, *orders()[:2], *orders()[2:])


def attend_kernel(normed, wq, wk, wv, q_out, k_out, v_out, mix_out, mix_turned):
    for out, weight in ((q_out, wq), (k_out, wk), (v_out, wv)):
        out[...] = dot(normed[...], weight[...]).astype(BF16)
    lane = lax.broadcasted_iota(jnp.int32, (128, 128), 1)
    masks = [lane // 32 == head for head in range(4)]
    edge = lax.axis_index("lat") == 0
    for w in range(6):
        rows = pl.ds(w * 128, 128)
        for group in range(2):
            lanes = pl.ds(group * 128, 128)
            scores = dot(q_out[rows, lanes], stack(k_out[rows, lanes], masks), NT)
            weights = jnp.exp(scores * SCALE)
            if w < 3:
                weights = jnp.where(other_region(128, 512, edge), 0.0, weights)
            pieces = []
            for head in range(4):
                piece = weights[:, head * 128:head * 128 + 128]
                pieces.append((piece * (1.0 / jnp.sum(piece, axis=-1, keepdims=True))).astype(BF16))
            mixture = select(dot(jnp.concatenate(pieces, axis=0), v_out[rows, lanes]), masks)
            mix_out[rows, lanes] = mixture.astype(BF16)
            mix_turned[lanes, rows] = mixture.T.astype(BF16)


def attend(normed, qkv_weight):
    tokens = jax.ShapeDtypeStruct((768, 1024), BF16)
    block = pl.BlockSpec((768, 256), lambda c: (0, c))
    weight = lambda third: pl.BlockSpec((1024, 256), lambda c: (0, third * 4 + c))
    return pl.pallas_call(
        attend_kernel,
        grid=(4,),
        out_shape=(tokens, tokens, tokens, tokens, jax.ShapeDtypeStruct((1024, 768), BF16)),
        in_specs=[pl.BlockSpec((768, 1024), lambda c: (0, 0)), weight(0), weight(1), weight(2)],
        out_specs=(block, block, block, block, pl.BlockSpec((256, 768), lambda c: (c, 0))),
        compiler_params=params(), name="attend",
    )(normed, qkv_weight, qkv_weight, qkv_weight)


def merge_kernel(x, mixture, merged_grad, out_weight, merge_weight, merged_out, grad_out, mixture_grad,
                 normed, total, normed_grad):
    step = pl.program_id(0)

    @pl.when(step == 0)
    def _():
        for w in range(6):
            rows = pl.ds(w * 128, 128)
            values = x[rows].astype(F32) + dot(mixture[rows], out_weight[...])
            values = values.astype(BF16).astype(F32)
            quarters = [values[32 * j:32 * j + 32] for j in range(4)]
            center = sum(jnp.sum(part, axis=-1, keepdims=True) for part in quarters) * (1 / 4096)
            quarters = [part - center for part in quarters]
            spread = sum(jnp.sum(jnp.square(part), axis=-1, keepdims=True) for part in quarters) * (1 / 4096)
            inverse = lax.rsqrt(spread + epsilon)
            for j in range(4):
                normed[j, pl.ds(w * 32, 32)] = quarters[j] * inverse
            total[1, pl.ds(w * 32, 32)] = jnp.broadcast_to(inverse, (32, 1024))
        total[0] = jnp.zeros((192, 1024), F32)

    total[0] += dot(normed[step].astype(BF16), merge_weight[...])
    normed_grad[step] = dot(merged_grad[...], merge_weight[...], NT).astype(BF16).astype(F32)

    @pl.when(step == 3)
    def _():
        merged_out[...] = total[0].astype(BF16)
        for w in range(6):
            part = pl.ds(w * 32, 32)
            first = sum(jnp.sum(normed_grad[j, part], axis=-1, keepdims=True) for j in range(4)) * (1 / 4096)
            second = sum(jnp.sum(normed_grad[j, part] * normed[j, part], axis=-1, keepdims=True)
                         for j in range(4)) * (1 / 4096)
            inverse = total[1, part]
            for j in range(4):
                value = inverse * (normed_grad[j, part] - first - normed[j, part] * second)
                grad_out[pl.ds(w * 128 + j * 32, 32)] = value.astype(BF16)
        mixture_grad[...] = dot(grad_out[...], out_weight[...], NT).astype(BF16)


def merge_both(x, mixture, merged_grad, out_weight, merge_weight):
    whole = lambda rows: pl.BlockSpec((rows, 1024), lambda j: (0, 0))
    tokens = jax.ShapeDtypeStruct((768, 1024), BF16)
    return pl.pallas_call(
        merge_kernel,
        grid=(4,),
        out_shape=(jax.ShapeDtypeStruct((192, 1024), BF16), tokens, tokens),
        in_specs=[whole(768), whole(768), whole(192), whole(1024), pl.BlockSpec((1024, 1024), lambda j: (j, 0))],
        out_specs=(whole(192), whole(768), whole(768)),
        scratch_shapes=[pltpu.VMEM((4, 192, 1024), F32), pltpu.VMEM((2, 192, 1024), F32),
                        pltpu.VMEM((4, 192, 1024), F32)],
        compiler_params=params(), name="merge_both",
    )(x, mixture, merged_grad, out_weight, merge_weight)


def shifted(block, axis, distance):
    devices = range(lax.axis_size(axis))
    route = [((i - distance) % len(devices), i) for i in devices]
    return lax.ppermute(block, axis, route)


def move_strips(grid_field, strip_width, offset):
    if offset == 1:
        outgoing = grid_field[:, :, -strip_width:]
    else:
        outgoing = grid_field[:, :, :strip_width]
    arrived = shifted(outgoing, "lon", offset)
    if offset == 1:
        middle = jnp.concatenate([arrived, grid_field[:, :, :-strip_width]], axis=2)
        outgoing_rows = middle[:, -strip_width:]
    else:
        middle = jnp.concatenate([grid_field[:, :, strip_width:], arrived], axis=2)
        outgoing_rows = middle[:, :strip_width]
    arrived_rows = shifted(outgoing_rows, "lat", offset)
    if offset == 1:
        return jnp.concatenate([arrived_rows, middle[:, :-strip_width]], axis=1)
    return jnp.concatenate([middle[:, strip_width:], arrived_rows], axis=1)


def to_groups(grid_field):
    return grid_field.reshape(2, 2, 4, 3, 4, 1024).transpose(1, 3, 0, 2, 4, 5).reshape(192, 1024)


def shards(tokens, qkv_weight, out_weight, merge_weight, merged_grad):
    framed = move_strips(tokens, SHIFT, 1)
    framed_merged_grad = move_strips(merged_grad, SHIFT // 2, 1)
    x, normed, normed_turned = prepare(framed, jnp.asarray(window_order(), BF16))
    q, k, v, mixture, mix_turned = attend(normed, qkv_weight)
    merged_groups, grad, mixture_grad = merge_both(x, mixture, to_groups(framed_merged_grad), out_weight, merge_weight)
    qkv_weight_grad, out_weight_grad, tokens_grad, merged = back(
        q, k, v, mixture, mixture_grad, normed_turned, mix_turned, grad, x, qkv_weight, merged_groups)
    return (merged.reshape(2, 8, 12, 1024), tokens_grad, qkv_weight_grad, out_weight_grad)


def solution(mesh):
    in_specs = (P(None, "lat", "lon", None), P(), P(), P(), P(None, "lat", "lon", None))
    out_specs = (
        P(None, "lat", "lon", None),
        P(None, "lat", "lon", None),
        P(("lat", "lon"), None),
        P(("lat", "lon"), None),
    )
    return jax.shard_map(shards, mesh=mesh, in_specs=in_specs, out_specs=out_specs, check_vma=False)
```

time: 1550 us -> 146 us (0.09)
  waiting for transfers between devices: 1150 us -> 12.6 us
  local copies, waits for them, and re-layouts: 201 us -> 7.98 us
  Pallas kernels: 0 us -> 114 us
  matrix products: 103 us -> 0 us
  other arithmetic: 50.8 us -> 3.05 us
    reduce_scatter x2 -> x0, waiting for transfers between devices: 1120 us -> none  [the longest x1 655 us: shards(): lax.psum_scatter(qkv_terms, ('lat', 'lon'), scatter_dimension=0, tiled=True)]
    pallas_call x0 -> x4, Pallas kernels: none -> 114 us  [the longest x1 72 us: back(): pl.pallas_call(back_kernel, out_shape=(jax.ShapeDtypeStruct((8, 3072), F3...]
    dot_general x14 -> x0, matrix products: 103 us -> none  [the longest x3 29.4 us: window_attention(): jnp.einsum('bqhd,bkhd->bhqk', queries, keys_part, preferred_element_type=...]
    reshape x7 -> x4, local copies, waits for them, and re-layouts: 65.4 us -> 2.5 us  [the longest x3 1.29 us: to_groups(): grid_field.reshape(2, 2, 4, 3, 4, 1024).transpose(1, 3, 0, 2, 4, 5)]
    unnamed x71 -> x14, local copies, waits for them, and re-layouts: 35.7 us -> 3.39 us
    convert_element_type x5 -> x0, local copies, waits for them, and re-layouts: 31.1 us -> none  [the longest x3 15.2 us: normalize(): values = grid_field.astype(jnp.float32)]
    add_any x1 -> x0, local copies, waits for them, and re-layouts: 25.8 us -> none  [window_attention(): queries = pieces[:, :, 0]]
    reduce_sum x6 -> x0, other arithmetic: 20.6 us -> none  [the longest x2 7.44 us: normalize(): center = jnp.mean(values, axis=-1, keepdims=True)]
  transfers between devices with their start and end apart: 10 -> 4, of which waited for: 8 -> 2; matrix products, arithmetic and copies ran while one was open for 12% -> 2% of each run, Pallas kernels for 0% -> 0%
where the time goes in v3:
time: 146 us; the launch traced here: 144 us
  Pallas kernels  114 us (78%)
  waiting for transfers between devices  12.6 us (9%)
  local copies, waits for them, and re-layouts  7.98 us (5%)
  starting transfers between devices  6.1 us (4%)
  other arithmetic  3.05 us (2%)
    pallas_call x1, Pallas kernels, back(): pl.pallas_call(back_kernel, out_shape=(jax.ShapeDtypeStruct((8, 3072), F3...  72 us
    pallas_call x1, Pallas kernels, attend(): pl.pallas_call(attend_kernel, grid=(4,), out_shape=(tokens, tokens, token...  19.5 us
    pallas_call x1, Pallas kernels, merge_both(): pl.pallas_call(merge_kernel, grid=(4,), out_shape=(jax.ShapeDtypeStruct((...  16 us
    ppermute x4, waiting for transfers between devices, shifted(): return lax.ppermute(block, axis, route)  12.6 us
    ppermute x4, starting transfers between devices, shifted(): return lax.ppermute(block, axis, route)  6.1 us
    pallas_call x1, Pallas kernels, prepare(): pl.pallas_call(prepare_kernel, grid=(6,), out_shape=(jax.ShapeDtypeStruct...  6.02 us
    unnamed x14, local copies, waits for them, and re-layouts  3.39 us
  transfers between devices with their start and end apart: 4, of which 2 were waited for; matrix products, arithmetic and copies ran while one was open for 2% of the time, Pallas kernels for 0%

profile of v3, /device:TPU:1, one launch (start us, length us, event | category | flops | bytes accessed | tf_op | source)
XLA Modules:
  0.0 144.0 jit_solution(18005887936753921623)
XLA Ops:
  0.6 0.0 copy-start.2
  0.6 1.2 slice.24
  1.9 2.7 %collective-permute-start = (bf16[2,16,4,1024]{3,2,1,0:T(4,128)(2,1)S(1)}, bf16[2,16,4,1024]{3,2,1,0:T(4,128)(2,1)S(1)}, u32[]{:S(2)}, u32[]{:S(2)}) collective-permute-start(bf16[2,16,4,1024]{3,2,1,0:T(4,128)(2,1)S(1)} %slice.24), channel_id=1, source_target_pairs={{15,0},{0,1},{1,2},{2,3},{3,4},{4,5},{5,6},{6,7},{7,8},{8,9},{9,10... | collective-permute-start | bytes 786440 | tf_op jit(solution)/shard_map/ppermute | solution.py:502
  4.5 0.8 slice.28
  5.4 0.0 collective-permute-start.2
  5.4 2.5 %collective-permute-done = bf16[2,16,4,1024]{3,2,1,0:T(4,128)(2,1)S(1)} collective-permute-done((bf16[2,16,4,1024]{3,2,1,0:T(4,128)(2,1)S(1)}, bf16[2,16,4,1024]{3,2,1,0:T(4,128)(2,1)S(1)}, u32[]{:S(2)}, u32[]{:S(2)}) %collective-permute-start) | collective-permute-done | bytes 262176 | tf_op jit(solution)/shard_map/ppermute | solution.py:502
  7.9 1.1 pad_maximum_fusion.2
  9.0 1.7 %collective-permute-start.1 = (bf16[2,4,24,1024]{3,2,1,0:T(8,128)(2,1)S(1)}, bf16[2,4,24,1024]{3,2,1,0:T(8,128)(2,1)S(1)}, u32[]{:S(2)}, u32[]{:S(2)}) collective-permute-start(bf16[2,4,24,1024]{3,2,1,0:T(8,128)(2,1)S(1)} %pad_maximum_fusion.2), channel_id=1, source_target_pairs={{112,0},{0,16},{16,32},{32,48},{48,64},{64,80},{80,96},{96,112},{1... | collective-permute-start | bytes 1179656 | tf_op jit(solution)/shard_map/ppermute | solution.py:502
  10.7 0.0 copy-done.2
  10.7 0.0 collective-permute-done.2
  10.7 0.1 pad_maximum_fusion.3
  10.9 0.0 copy-start
  10.9 1.7 %collective-permute-start.3 = (bf16[2,2,12,1024]{3,1,2,0:T(2,128)(2,1)S(1)}, bf16[2,2,12,1024]{3,1,2,0:T(2,128)(2,1)S(1)}, u32[]{:S(2)}, u32[]{:S(2)}) collective-permute-start(bf16[2,2,12,1024]{3,1,2,0:T(2,128)(2,1)S(1)} %pad_maximum_fusion.3), channel_id=1, source_target_pairs={{112,0},{0,16},{16,32},{32,48},{48,64},{64,80},{80,96},{96,112},{1... | collective-permute-start | bytes 294920 | tf_op jit(solution)/shard_map/ppermute | solution.py:502
  12.6 10.2 %collective-permute-done.3 = bf16[2,2,12,1024]{3,1,2,0:T(2,128)(2,1)S(1)} collective-permute-done((bf16[2,2,12,1024]{3,1,2,0:T(2,128)(2,1)S(1)}, bf16[2,2,12,1024]{3,1,2,0:T(2,128)(2,1)S(1)}, u32[]{:S(2)}, u32[]{:S(2)}) %collective-permute-start.3) | collective-permute-done | bytes 98336 | tf_op jit(solution)/shard_map/ppermute | solution.py:502
  22.7 0.2 fusion.1
  22.9 0.1 reshape.17
  23.1 0.3 copy.19
  23.4 0.8 reshape.18.merged_grad
  24.2 0.0 collective-permute-done.1
  24.2 0.0 copy-done
  24.2 1.7 %fusion.framed = bf16[2,16,24,1024]{3,2,1,0:T(8,128)(2,1)} fusion(bf16[2,16,20,1024]{3,2,1,0:T(8,128)(2,1)S(1)} %bitcast.9, bf16[2,16,4,1024]{3,2,1,0:T(4,128)(2,1)S(1)} %collective-permute-done, bf16[2,4,24,1024]{3,2,1,0:T(8,128)(2,1)S(1)} %collective-permute-done.1), kind=kLoop, calls=%fused_computation.1 | loop fusion | flops 4718592 | bytes 3538944 | tf_op jit(solution)/shard_map/concatenate | solution.py:519
  25.9 6.0 %prepare.1 = (bf16[768,1024]{1,0:T(8,128)(2,1)}, bf16[768,1024]{1,0:T(8,128)(2,1)}, bf16[1024,768]{1,0:T(8,128)(2,1)}) custom-call(bf16[2,16,24,1024]{3,2,1,0:T(8,128)(2,1)} %fusion.framed, bf16[128,128]{1,0:T(8,128)(2,1)} %constant.10.clone.order), custom_call_target="tpu_custom_call" | custom-call | tf_op jit(solution)/shard_map/prepare/pallas_call | solution.py:72
  31.9 19.5 %attend.1 = (bf16[768,1024]{1,0:T(8,128)(2,1)}, bf16[768,1024]{1,0:T(8,128)(2,1)}, bf16[768,1024]{1,0:T(8,128)(2,1)}, bf16[768,1024]{1,0:T(8,128)(2,1)}, bf16[1024,768]{1,0:T(8,128)(2,1)}) custom-call(bf16[768,1024]{1,0:T(8,128)(2,1)} %get-tuple-element.19.normed, bf16[1024,3072]{1,0:T(8,128)(2,1)} %weight_hbm.1, bf16[1024,3072]{1,0:T(8,128)(2,1)} %weight_hbm.1, ...), custom_call_target="tpu_custom_call" | custom-call | tf_op jit(solution)/shard_map/attend/pallas_call | solution.py:436
  51.4 16.0 %merge_both.1 = (bf16[192,1024]{1,0:T(8,128)(2,1)}, bf16[768,1024]{1,0:T(8,128)(2,1)}, bf16[768,1024]{1,0:T(8,128)(2,1)}) custom-call(bf16[768,1024]{1,0:T(8,128)(2,1)} %get-tuple-element.24.x.x_hbm, bf16[768,1024]{1,0:T(8,128)(2,1)} %get-tuple-element.23.mixture.mix_hbm, bf16[192,1024]{1,0:T(8,128)(2,1)} %reshape.18.merged_grad, ...), custom_call_target="tpu_custom_call" | custom-call | tf_op jit(solution)/shard_map/merge_both/pallas_call | solution.py:487
  67.4 72.0 %back.1 = (f32[8,3072]{1,0:T(8,128)}, f32[8,1024]{1,0:T(8,128)}, bf16[2,16,24,1024]{3,2,1,0:T(8,128)(2,1)}, bf16[192,1024]{1,0:T(8,128)(2,1)}) custom-call(bf16[768,1024]{1,0:T(8,128)(2,1)} %get-tuple-element.20.q_hbm, bf16[768,1024]{1,0:T(8,128)(2,1)} %get-tuple-element.21.k_hbm, bf16[768,1024]{1,0:T(8,128)(2,1)} %get-tuple-element.22.v_hbm, ...), custom_call_target="tpu_custom_call" | custom-call | tf_op jit(solution)/shard_map/back/pallas_call | solution.py:378
  139.4 0.0 copy-start.1
  139.4 1.2 reshape.19
  140.6 1.0 copy.17
  141.6 0.0 copy-done.1
  141.6 1.1 copy.23
  142.8 0.6 copy.24
  143.4 0.6 copy.25
  (5 shorter events, 0.0 us)
Async XLA Ops:
  0.6 10.1 %copy-start.2 = (bf16[2,8,12,1024]{3,1,2,0:T(8,128)(2,1)S(1)}, bf16[2,8,12,1024]{3,1,2,0:T(8,128)(2,1)}, u32[]{:S(2)}) copy-start(bf16[2,8,12,1024]{3,1,2,0:T(8,128)(2,1)} %param.14) | copy-start | bytes 1179652
  1.9 6.0 %collective-permute-start = (bf16[2,16,4,1024]{3,2,1,0:T(4,128)(2,1)S(1)}, bf16[2,16,4,1024]{3,2,1,0:T(4,128)(2,1)S(1)}, u32[]{:S(2)}, u32[]{:S(2)}) collective-permute-start(bf16[2,16,4,1024]{3,2,1,0:T(4,128)(2,1)S(1)} %slice.24), channel_id=1, source_target_pairs={{15,0},{0,1},{1,2},{2,3},{3,4},{4,5},{5,6},{6,7},{7,8},{8,9},{9,10... | collective-permute-start | bytes 786440 | tf_op jit(solution)/shard_map/ppermute | solution.py:502
  5.4 5.3 %collective-permute-start.2 = (bf16[2,8,2,1024]{3,1,2,0:T(8,128)(2,1)S(1)}, bf16[2,8,2,1024]{3,1,2,0:T(8,128)(2,1)S(1)}, u32[]{:S(2)}, u32[]{:S(2)}) collective-permute-start(bf16[2,8,2,1024]{3,1,2,0:T(8,128)(2,1)S(1)} %slice.28), channel_id=1, source_target_pairs={{15,0},{0,1},{1,2},{2,3},{3,4},{4,5},{5,6},{6,7},{7,8},{8,9},{9,10... | collective-permute-start | bytes 196616 | tf_op jit(solution)/shard_map/ppermute | solution.py:502
  9.0 15.2 %collective-permute-start.1 = (bf16[2,4,24,1024]{3,2,1,0:T(8,128)(2,1)S(1)}, bf16[2,4,24,1024]{3,2,1,0:T(8,128)(2,1)S(1)}, u32[]{:S(2)}, u32[]{:S(2)}) collective-permute-start(bf16[2,4,24,1024]{3,2,1,0:T(8,128)(2,1)S(1)} %pad_maximum_fusion.2), channel_id=1, source_target_pairs={{112,0},{0,16},{16,32},{32,48},{48,64},{64,80},{80,96},{96,112},{1... | collective-permute-start | bytes 1179656 | tf_op jit(solution)/shard_map/ppermute | solution.py:502
  10.9 13.4 %copy-start = (bf16[2,16,24,1024]{3,2,1,0:T(8,128)(2,1)S(1)}, bf16[2,16,24,1024]{3,2,1,0:T(8,128)(2,1)}, u32[]{:S(2)}) copy-start(bf16[2,16,24,1024]{3,2,1,0:T(8,128)(2,1)} %param.10) | copy-start | bytes 4718596
  10.9 11.9 %collective-permute-start.3 = (bf16[2,2,12,1024]{3,1,2,0:T(2,128)(2,1)S(1)}, bf16[2,2,12,1024]{3,1,2,0:T(2,128)(2,1)S(1)}, u32[]{:S(2)}, u32[]{:S(2)}) collective-permute-start(bf16[2,2,12,1024]{3,1,2,0:T(2,128)(2,1)S(1)} %pad_maximum_fusion.3), channel_id=1, source_target_pairs={{112,0},{0,16},{16,32},{32,48},{48,64},{64,80},{80,96},{96,112},{1... | collective-permute-start | bytes 294920 | tf_op jit(solution)/shard_map/ppermute | solution.py:502
  139.4 2.2 %copy-start.1 = (bf16[2,16,24,1024]{3,2,1,0:T(8,128)(2,1)S(1)}, bf16[2,16,24,1024]{3,2,1,0:T(8,128)(2,1)}, u32[]{:S(2)}) copy-start(bf16[2,16,24,1024]{3,2,1,0:T(8,128)(2,1)} %get-tuple-element.47) | copy-start | bytes 4718596
  141.6 1.1 copy-start.3
  141.6 1.8 %copy-start.4 = (f32[8,1024]{1,0:T(8,128)S(1)}, f32[8,1024]{1,0:T(8,128)}, u32[]{:S(2)}) copy-start(f32[8,1024]{1,0:T(8,128)} %get-tuple-element.49) | copy-start | bytes 98308

commit v4 on v3

--- a/solution.py
+++ b/solution.py
@@ -6,10 +6,7 @@
 from jax.experimental.pallas import tpu as pltpu
 from jax.sharding import PartitionSpec as P
 
-SHIFT = 4
 CHUNKS = 4
-LANES = 512
-WIDTH = 256
 MESH = pl.DeviceIdType.MESH
 F32, BF16 = jnp.float32, jnp.bfloat16
 epsilon = 1e-05
@@ -58,30 +55,6 @@
     return shifted_values, lax.rsqrt(spread + epsilon)
 
 
-def prepare_kernel(framed, order, x_out, normed_out, normed_turned):
-    natural = framed[...].astype(F32).reshape(128, 1024).astype(BF16)
-    values = dot(order[...], natural)
-    x_out[...] = values.astype(BF16)
-    centered, inverse = statistics(values)
-    normed = centered * inverse
-    normed_out[...] = normed.astype(BF16)
-    normed_turned[...] = normed.T.astype(BF16)
-
-
-def prepare(framed, order):
-    return pl.pallas_call(
-        prepare_kernel,
-        grid=(6,),
-        out_shape=(jax.ShapeDtypeStruct((768, 1024), BF16), jax.ShapeDtypeStruct((768, 1024), BF16),
-                   jax.ShapeDtypeStruct((1024, 768), BF16)),
-        in_specs=[pl.BlockSpec((2, 8, 8, 1024), lambda w: (0, w // 3, w % 3, 0)),
-                  pl.BlockSpec((128, 128), lambda w: (0, 0))],
-        out_specs=(pl.BlockSpec((128, 1024), lambda w: (w, 0)), pl.BlockSpec((128, 1024), lambda w: (w, 0)),
-                   pl.BlockSpec((1024, 128), lambda w: (0, w))),
-        compiler_params=params(), name="prepare",
-    )(framed, order)
-
-
 def place():
     lat, lon = lax.axis_index("lat"), lax.axis_index("lon")
     return (lat // 4) * 2 + (lon // 2) % 2, lon // 4, lat % 4, lon % 2
@@ -149,15 +122,14 @@
         loads[name] = pltpu.make_async_copy(source, target, load.at[index])
         loads[name].start()
 
+    fetch("mix", 21, mix_turned_hbm, mix_turned)
+    fetch("grad", 22, grad_hbm, grad)
+    fetch("normed", 20, normed_hbm, normed_turned)
     wide = ((q_hbm, q), (k_hbm, k), (v_hbm, v), (mix_hbm, mix), (mix_grad_hbm, mix_grad))
     for chunk in range(CHUNKS):
         columns = pl.ds(chunk * 256, 256)
         for i, (source, target) in enumerate(wide):
             fetch((chunk, i), chunk * 5 + i, source.at[:, columns], target.at[:, columns])
-        if chunk == 0:
-            fetch("normed", 20, normed_hbm, normed_turned)
-            fetch("mix", 21, mix_turned_hbm, mix_turned)
-            fetch("grad", 22, grad_hbm, grad)
     fetch("weight", 23, weight_hbm, qkv_weight)
     fetch("x", 24, x_hbm, x_in)
 
@@ -175,6 +147,7 @@
     greet(ring + list(after), ring + list(before))
 
     started = []
+    first_send = {}
 
     def push(copy):
         copy.start()
@@ -188,14 +161,14 @@
     for copy in merged_copies:
         push(copy)
 
-    def run(stream):
-        chunk, part = stream // 2, stream % 2
-        slot = chunk % 2
-        lanes = pl.ds(part * WIDTH, WIDTH)
-        order = [(stream + i) % 3 for i in range(3)]
+    def run(kind, chunk):
+        stream = kind * CHUNKS + chunk
+        slot = 6 + chunk if kind == 3 else chunk % 2 * 3 + kind
+        order = [(kind + chunk + i) % 3 for i in range(3)]
         mine = [here[axis] for axis in order]
-        copy = push(remote(g.at[slot, :, 1 - core, :, lanes], from_core.at[stream],
-                           send.at[stream, 0], recv.at[stream, 0], sibling))
+        copy = remote(g.at[slot, :, 1 - core], from_core.at[stream], send.at[stream, 0], recv.at[stream, 0], sibling)
+        copy.start()
+        first_send[(kind, chunk)] = copy
         yield
         copy.wait_recv()
 
@@ -206,7 +179,7 @@
                 for axis, value in zip(order, (a, b, c)):
                     at[axis] = value
                 row = ((at[0] // 2) * 4 + at[2]) * 8 + at[1] * 2 + at[0] % 2
-                total = g[slot, row, core, :, lanes].astype(F32) + from_core[stream, row].astype(F32)
+                total = g[slot, row, core].astype(F32) + from_core[stream, row].astype(F32)
                 acc_a[stream, a, b * 4 + c] = total.astype(BF16)
             return carry
 
@@ -228,13 +201,9 @@
             elif level == 1:
                 for i in range(4):
                     acc_c[stream, i] = total[i].astype(BF16)
-        columns = WIDTH * chunk
-        if part == 0:
-            qkv_out[:, columns:columns + WIDTH] = total[:8]
-            qkv_out[:, 2048 + columns:2048 + columns + WIDTH] = total[8:]
-        else:
-            qkv_out[:, 1024 + columns:1024 + columns + WIDTH] = total[:8]
-            out_out[:, columns:columns + WIDTH] = total[8:]
+        target, base = (out_out, chunk * 256) if kind == 3 else (qkv_out, kind * 1024 + chunk * 256)
+        target[:, base:base + 128] = total[:8]
+        target[:, base + 128:base + 256] = total[8:]
 
     running = []
 
@@ -250,7 +219,28 @@
     lane8 = lax.broadcasted_iota(jnp.int32, (8, 256), 1) // 32
     own_head = jnp.where(lane8 == row8, 1.0, 0.0).astype(BF16)
     edge = lax.axis_index("lat") == 0
-    first_send = {}
+    def weight_terms(kinds, chunk):
+        def weight_rows(i, carry):
+            rows = pl.ds(pl.multiple_of(i * 256, 256), 256)
+            pairs = pl.ds(i * 16, 16)
+            for kind in kinds:
+                left, right = ((normed_turned, dq), (normed_turned, dk), (normed_turned, dv), (mix_turned, grad))[kind]
+                terms = dot(left[rows], right[:, chunk * 256:chunk * 256 + 256]).reshape(32, 8, 256)
+                both = jnp.concatenate([terms[:, :, :128], terms[:, :, 128:]], axis=1)
+                slot = 6 + chunk if kind == 3 else chunk % 2 * 3 + kind
+                g[slot, pairs] = both.astype(BF16).reshape(16, 2, 16, 128)
+            return carry
+
+        lax.fori_loop(0, 4, weight_rows, 0)
+        for kind in kinds:
+            job = run(kind, chunk)
+            next(job)
+            running.append(job)
+
+    for name in ("normed", "mix", "grad"):
+        loads[name].wait()
+    for chunk in range(CHUNKS):
+        weight_terms((3,), chunk)
     for chunk in range(CHUNKS):
         columns = slice(chunk * 256, chunk * 256 + 256)
         for i in range(5):
@@ -286,33 +276,11 @@
                 dq[rows, columns] = (jnp.concatenate(pieces, axis=0).T * SCALE).astype(BF16)
 
         pl.loop(0, 2)(window_back)
-        if chunk == 0:
-            for name in ("normed", "mix", "grad"):
-                loads[name].wait()
-        slot = chunk % 2
+        advance()
         if chunk >= 2:
-            for copy in first_send[chunk - 2]:
-                copy.wait_send()
-
-        def weight_rows(i, carry):
-            rows = pl.ds(pl.multiple_of(i * 256, 256), 256)
-            pairs = pl.ds(i * 16, 16)
-            normed_part = normed_turned[rows]
-            for part, (upper, lower) in enumerate((
-                    (dot(normed_part, dq[:, columns]), dot(normed_part, dv[:, columns])),
-                    (dot(normed_part, dk[:, columns]), dot(mix_turned[rows], grad[:, columns])))):
-                both = jnp.concatenate([upper.reshape(32, 8, 256), lower.reshape(32, 8, 256)], axis=1)
-                g[slot, pairs, :, :, part * WIDTH:part * WIDTH + WIDTH] = both.astype(BF16).reshape(16, 2, 16, 256)
-            return carry
-
-        lax.fori_loop(0, 4, weight_rows, 0)
-        advance()
-        for part in range(2):
-            job = run(2 * chunk + part)
-            next(job)
-            running.append(job)
-        first_send[chunk] = started[-2:]
-        del started[-2:]
+            for kind in range(3):
+                first_send.pop((kind, chunk - 2)).wait_send()
+        weight_terms((0, 1, 2), chunk)
     loads["weight"].wait()
     loads["x"].wait()
 
@@ -338,7 +306,7 @@
             normed_grad[tokens, rows] = (dot(dq[tokens], qkv_weight[rows, 0:1024], NT)
                                          + dot(dk[tokens], qkv_weight[rows, 1024:2048], NT)
                                          + dot(dv[tokens], qkv_weight[rows, 2048:3072], NT))
-            if i % 2 == 1 and (half, i) != (1, 1):
+            if (half, i) in ((0, 1), (1, 3)):
                 advance()
         for wb in range(3):
             finish_window(half * 3 + wb)
@@ -347,11 +315,13 @@
         if half == 0:
             push(strips[0])
             push(strips[2])
+        advance()
     for copy in merged_copies:
         copy.wait_recv()
     merged_natural_units = jnp.concatenate([merged_units[i, 1:7].reshape(48, 1024) for i in range(1, 5)], axis=0)
-    merged_out[...] = dot(merged_natural[...], merged_natural_units.astype(BF16)).astype(BF16)
-    advance()
+    natural = dot(merged_natural[...], merged_natural_units.astype(BF16))
+    for i in range(16):
+        merged_out[i // 8, i % 8] = natural[12 * i:12 * i + 12].astype(BF16)
     for copy in strips:
         copy.wait_recv()
     for m in range(2):
@@ -363,38 +333,35 @@
         tokens_out[:, 8 * m:8 * m + 8] = jnp.concatenate(blocks, axis=2).astype(BF16)
     while running:
         advance()
-    for chunk in range(2, CHUNKS):
-        for copy in first_send[chunk]:
-            copy.wait_send()
-    for copy in started:
+    for copy in list(first_send.values()) + started:
         copy.wait_send()
 
 
 def back(q, k, v, mix, mix_grad, normed_turned, mix_turned, grad, x, qkv_weight, merged_groups):
-    streams = 2 * CHUNKS
+    streams = 4 * CHUNKS
     vmem, anywhere = pl.BlockSpec(memory_space=pltpu.VMEM), pl.BlockSpec(memory_space=pl.ANY)
     tokens = pltpu.VMEM((768, 1024), BF16)
     turned = pltpu.VMEM((1024, 768), BF16)
     return pl.pallas_call(
         back_kernel,
         out_shape=(jax.ShapeDtypeStruct((8, 3072), F32), jax.ShapeDtypeStruct((8, 1024), F32),
-                   jax.ShapeDtypeStruct((2, 16, 24, 1024), BF16), jax.ShapeDtypeStruct((192, 1024), BF16)),
+                   jax.ShapeDtypeStruct((2, 16, 24, 1024), BF16), jax.ShapeDtypeStruct((2, 8, 12, 1024), BF16)),
         in_specs=[anywhere] * 10 + [vmem] * 5,
         out_specs=(vmem, vmem, vmem, vmem),
         scratch_shapes=[
             tokens, tokens, tokens, tokens, tokens, turned, turned, tokens, tokens, pltpu.VMEM((1024, 3072), BF16),
             tokens, tokens, tokens,
-            pltpu.VMEM((2, 64, 2, 16, LANES), BF16),
+            pltpu.VMEM((10, 64, 2, 16, 128), BF16),
             pltpu.VMEM((768, 1024), F32),
             pltpu.VMEM((5, 7, 32, 1024), BF16),
             pltpu.VMEM((5, 7, 8, 1024), F32),
-            pltpu.VMEM((streams, 64, 16, WIDTH), BF16),
-            pltpu.VMEM((streams, 4, 16, 16, WIDTH), BF16),
-            pltpu.VMEM((streams, 3, 16, 16, WIDTH), BF16),
-            pltpu.VMEM((streams, 4, 4, 16, WIDTH), BF16),
-            pltpu.VMEM((streams, 3, 4, 16, WIDTH), BF16),
-            pltpu.VMEM((streams, 4, 16, WIDTH), BF16),
-            pltpu.VMEM((streams, 3, 16, WIDTH), BF16),
+            pltpu.VMEM((streams, 64, 16, 128), BF16),
+            pltpu.VMEM((streams, 4, 16, 16, 128), BF16),
+            pltpu.VMEM((streams, 3, 16, 16, 128), BF16),
+            pltpu.VMEM((streams, 4, 4, 16, 128), BF16),
+            pltpu.VMEM((streams, 3, 4, 16, 128), BF16),
+            pltpu.VMEM((streams, 4, 16, 128), BF16),
+            pltpu.VMEM((streams, 3, 16, 128), BF16),
             pltpu.SemaphoreType.DMA((25,)),
             pltpu.SemaphoreType.DMA((streams, 10)),
             pltpu.SemaphoreType.DMA((streams, 10)),
@@ -403,7 +370,80 @@
         ],
         compiler_params=pltpu.CompilerParams(collective_id=0, has_side_effects=True, vmem_limit_bytes=62 * MIB),
         name="back",
-    )(q, k, v, mix, mix_grad, normed_turned, mix_turned, grad, x, qkv_weight, merged_groups, *orders()[:2], *orders()[2:])
+    )(q, k, v, mix, mix_grad, normed_turned, mix_turned, grad, x, qkv_weight, merged_groups, *orders())
+
+
+def enter_kernel(tokens, merged_grad, to_natural, to_quarters, merged_natural, merged_windows,
+                 x_out, normed_out, normed_turned, groups_out, units, merged_units, send, recv):
+    before, after = neighbours(-1), neighbours(1)
+    greet(before, after)
+    copies = (frame_copies(units, (4, 6), (0, 0), send, recv, 0, after)
+              + frame_copies(merged_units, (4, 6), (0, 0), send, recv, 3, after))
+    for m in (1, 0):
+        rows = tokens[:, 8 * m:8 * m + 8].astype(F32)
+        for n in range(3):
+            natural = rows[:, :, 8 * n:8 * n + 8].reshape(128, 1024).astype(BF16)
+            quarters = dot(to_natural[...], natural, TN).astype(BF16).reshape(4, 32, 1024)
+            for u in range(2):
+                for side in range(2):
+                    units[2 * m + 1 + u, 2 * n + 1 + side] = quarters[2 * u + side]
+        if m == 1:
+            copies[0].start()
+            copies[2].start()
+        else:
+            copies[1].start()
+    merged_in = dot(merged_natural[...], merged_grad[...], TN).reshape(4, 6, 8, 1024)
+    for i in range(4):
+        merged_units[i + 1, 1:7] = merged_in[i]
+    for copy in copies[3:]:
+        copy.start()
+
+    def window(w):
+        wa, wb = w // 3, w % 3
+        quarters = [units[2 * wa + u, 2 * wb + side] for u in range(2) for side in range(2)]
+        values = dot(to_quarters[...], jnp.concatenate(quarters, axis=0))
+        rows = pl.ds(w * 128, 128)
+        x_out[rows] = values.astype(BF16)
+        centered, inverse = statistics(values)
+        normed = centered * inverse
+        normed_out[rows] = normed.astype(BF16)
+        normed_turned[:, rows] = normed.T.astype(BF16)
+
+    window(4)
+    window(5)
+    copies[1].wait_recv()
+    window(3)
+    for copy in copies[3:]:
+        copy.wait_recv()
+    groups = jnp.concatenate([merged_units[i, 0:6].reshape(48, 1024) for i in range(4)], axis=0)
+    groups_out[...] = dot(merged_windows[...], groups.astype(BF16)).astype(BF16)
+    copies[0].wait_recv()
+    window(1)
+    window(2)
+    copies[2].wait_recv()
+    window(0)
+    for copy in copies:
+        copy.wait_send()
+
+
+def enter(tokens, merged_grad):
+    vmem = pl.BlockSpec(memory_space=pltpu.VMEM)
+    grid_tokens = jax.ShapeDtypeStruct((768, 1024), BF16)
+    return pl.pallas_call(
+        enter_kernel,
+        out_shape=(grid_tokens, grid_tokens, jax.ShapeDtypeStruct((1024, 768), BF16),
+                   jax.ShapeDtypeStruct((192, 1024), BF16)),
+        in_specs=[vmem] * 6,
+        out_specs=(vmem,) * 4,
+        scratch_shapes=[
+            pltpu.VMEM((5, 7, 32, 1024), BF16),
+            pltpu.VMEM((5, 7, 8, 1024), F32),
+            pltpu.SemaphoreType.DMA((6,)),
+            pltpu.SemaphoreType.DMA((6,)),
+        ],
+        compiler_params=pltpu.CompilerParams(collective_id=1, has_side_effects=True, vmem_limit_bytes=48 * MIB),
+        name="enter",
+    )(tokens, merged_grad, *orders())
 
 
 def attend_kernel(normed, wq, wk, wv, q_out, k_out, v_out, mix_out, mix_turned):
@@ -496,43 +536,13 @@
     )(x, mixture, merged_grad, out_weight, merge_weight)
 
 
-def shifted(block, axis, distance):
-    devices = range(lax.axis_size(axis))
-    route = [((i - distance) % len(devices), i) for i in devices]
-    return lax.ppermute(block, axis, route)
-
-
-def move_strips(grid_field, strip_width, offset):
-    if offset == 1:
-        outgoing = grid_field[:, :, -strip_width:]
-    else:
-        outgoing = grid_field[:, :, :strip_width]
-    arrived = shifted(outgoing, "lon", offset)
-    if offset == 1:
-        middle = jnp.concatenate([arrived, grid_field[:, :, :-strip_width]], axis=2)
-        outgoing_rows = middle[:, -strip_width:]
-    else:
-        middle = jnp.concatenate([grid_field[:, :, strip_width:], arrived], axis=2)
-        outgoing_rows = middle[:, :strip_width]
-    arrived_rows = shifted(outgoing_rows, "lat", offset)
-    if offset == 1:
-        return jnp.concatenate([arrived_rows, middle[:, :-strip_width]], axis=1)
-    return jnp.concatenate([middle[:, strip_width:], arrived_rows], axis=1)
-
-
-def to_groups(grid_field):
-    return grid_field.reshape(2, 2, 4, 3, 4, 1024).transpose(1, 3, 0, 2, 4, 5).reshape(192, 1024)
-
-
 def shards(tokens, qkv_weight, out_weight, merge_weight, merged_grad):
-    framed = move_strips(tokens, SHIFT, 1)
-    framed_merged_grad = move_strips(merged_grad, SHIFT // 2, 1)
-    x, normed, normed_turned = prepare(framed, jnp.asarray(window_order(), BF16))
+    x, normed, normed_turned, merged_grad_groups = enter(tokens, merged_grad.reshape(192, 1024))
     q, k, v, mixture, mix_turned = attend(normed, qkv_weight)
-    merged_groups, grad, mixture_grad = merge_both(x, mixture, to_groups(framed_merged_grad), out_weight, merge_weight)
+    merged_groups, grad, mixture_grad = merge_both(x, mixture, merged_grad_groups, out_weight, merge_weight)
     qkv_weight_grad, out_weight_grad, tokens_grad, merged = back(
         q, k, v, mixture, mixture_grad, normed_turned, mix_turned, grad, x, qkv_weight, merged_groups)
-    return (merged.reshape(2, 8, 12, 1024), tokens_grad, qkv_weight_grad, out_weight_grad)
+    return (merged, tokens_grad, qkv_weight_grad, out_weight_grad)
 
 
 def solution(mesh):

time: 146 us -> 142 us (0.973)
  Pallas kernels: 114 us -> 129 us
  waiting for transfers between devices: 12.6 us -> 0 us
  starting transfers between devices: 6.1 us -> 0 us
  local copies, waits for them, and re-layouts: 7.98 us -> 11.7 us
  other arithmetic: 3.05 us -> 0 us
    pallas_call x1, Pallas kernels: 6.02 us -> 26.4 us  [enter(): pl.pallas_call(enter_kernel, out_shape=(grid_tokens, grid_tokens, jax.Sha...]
    ppermute x4 -> x0, waiting for transfers between devices: 12.6 us -> none  [shifted(): return lax.ppermute(block, axis, route)]
    unnamed x14 -> x25, local copies, waits for them, and re-layouts: 3.39 us -> 11.6 us
    ppermute x4 -> x0, starting transfers between devices: 6.1 us -> none  [shifted(): return lax.ppermute(block, axis, route)]
    pallas_call x1, Pallas kernels: 72 us -> 67.1 us  [back(): pl.pallas_call(back_kernel, out_shape=(jax.ShapeDtypeStruct((8, 3072), F3...]
    reshape x4 -> x1, local copies, waits for them, and re-layouts: 2.5 us -> 0.09 us  [shards(): merged_grad.reshape(192, 1024)]
    slice x3 -> x0, local copies, waits for them, and re-layouts: 2.1 us -> none  [the longest x2 2.08 us: move_strips(): outgoing = grid_field[:, :, -strip_width:]]
    concatenate x2 -> x0, other arithmetic: 1.83 us -> none  [move_strips(): return jnp.concatenate([arrived_rows, middle[:, :-strip_width]], axis=1)]
  transfers between devices with their start and end apart: 4 -> 0, of which waited for: 2 -> 0; matrix products, arithmetic and copies ran while one was open for 2% -> 0% of each run, Pallas kernels for 0% -> 0%
where the time goes in v4:
time: 142 us; the launch traced here: 141 us
  Pallas kernels  129 us (91%)
  local copies, waits for them, and re-layouts  11.7 us (8%)
    pallas_call x1, Pallas kernels, back(): pl.pallas_call(back_kernel, out_shape=(jax.ShapeDtypeStruct((8, 3072), F3...  67.1 us
    pallas_call x1, Pallas kernels, enter(): pl.pallas_call(enter_kernel, out_shape=(grid_tokens, grid_tokens, jax.Sha...  26.4 us
    pallas_call x1, Pallas kernels, attend(): pl.pallas_call(attend_kernel, grid=(4,), out_shape=(tokens, tokens, token...  19.5 us
    pallas_call x1, Pallas kernels, merge_both(): pl.pallas_call(merge_kernel, grid=(4,), out_shape=(jax.ShapeDtypeStruct((...  16 us
    unnamed x25, local copies, waits for them, and re-layouts  11.6 us

profile of v4, /device:TPU:1, one launch (start us, length us, event | category | flops | bytes accessed | tf_op | source)
XLA Modules:
  0.0 141.5 jit_solution(994174199535073367)
XLA Ops:
  0.6 0.0 copy-start.3
  0.6 0.0 copy-start.4
  0.7 0.0 copy-start.6
  0.7 0.0 copy-start.7
  0.7 1.3 copy.19
  2.0 0.1 reshape.11.merged_grad
  2.1 0.0 copy-done.3
  2.1 0.0 copy-done.4
  2.1 0.0 copy-done.6
  2.1 0.0 copy-done.7
  2.1 26.4 %enter.1 = (bf16[768,1024]{1,0:T(8,128)(2,1)S(1)}, bf16[768,1024]{1,0:T(8,128)(2,1)S(1)}, bf16[1024,768]{1,0:T(8,128)(2,1)S(1)}, bf16[192,1024]{1,0:T(8,128)(2,1)S(1)}) custom-call(bf16[2,16,24,1024]{3,2,1,0:T(8,128)(2,1)} %tokens.1, bf16[192,1024]{1,0:T(8,128)(2,1)S(1)} %reshape.11.merged_grad, bf16[128,128]{1,0:T(8,128)(2,1)S(1)} %copy-done.7, ...), custom_call_target="tpu_custom_call" | custom-call | tf_op jit(solution)/shard_map/enter/pallas_call | solution.py:432
  28.5 0.0 copy-start
  28.5 1.2 copy-done
  29.8 0.0 copy-start.1
  29.8 1.2 copy-done.1
  31.0 0.0 copy-start.2
  31.0 1.1 copy-done.2
  32.1 0.0 copy-start.5
  32.1 0.7 copy-done.5
  32.9 19.5 %attend.1 = (bf16[768,1024]{1,0:T(8,128)(2,1)}, bf16[768,1024]{1,0:T(8,128)(2,1)}, bf16[768,1024]{1,0:T(8,128)(2,1)}, bf16[768,1024]{1,0:T(8,128)(2,1)}, bf16[1024,768]{1,0:T(8,128)(2,1)}) custom-call(bf16[768,1024]{1,0:T(8,128)(2,1)} %copy-done.2, bf16[1024,3072]{1,0:T(8,128)(2,1)} %weight_hbm.1, bf16[1024,3072]{1,0:T(8,128)(2,1)} %weight_hbm.1, ...), custom_call_target="tpu_custom_call" | custom-call | tf_op jit(solution)/shard_map/attend/pallas_call | solution.py:476
  52.4 16.0 %merge_both.1 = (bf16[192,1024]{1,0:T(8,128)(2,1)}, bf16[768,1024]{1,0:T(8,128)(2,1)}, bf16[768,1024]{1,0:T(8,128)(2,1)}) custom-call(bf16[768,1024]{1,0:T(8,128)(2,1)} %copy-done, bf16[768,1024]{1,0:T(8,128)(2,1)} %get-tuple-element.24.mixture.mix_hbm, bf16[192,1024]{1,0:T(8,128)(2,1)} %copy-done.5, bf16[1024,1024]{1,0:T(8,128)(2,1)} %out_weight.1, ...), custom_call_target="tpu_custom_call" | custom-call | tf_op jit(solution)/shard_map/merge_both/pallas_call | solution.py:527
  68.4 67.1 %back.1 = (f32[8,3072]{1,0:T(8,128)}, f32[8,1024]{1,0:T(8,128)}, bf16[2,16,24,1024]{3,2,1,0:T(8,128)(2,1)}, bf16[2,8,12,1024]{3,2,1,0:T(8,128)(2,1)}) custom-call(bf16[768,1024]{1,0:T(8,128)(2,1)} %get-tuple-element.21.q_hbm, bf16[768,1024]{1,0:T(8,128)(2,1)} %get-tuple-element.22.k_hbm, bf16[768,1024]{1,0:T(8,128)(2,1)} %get-tuple-element.23.v_hbm, ...), custom_call_target="tpu_custom_call" | custom-call | tf_op jit(solution)/shard_map/back/pallas_call | solution.py:345
  135.5 2.0 %copy.20 = bf16[2,8,12,1024]{3,1,2,0:T(8,128)(2,1)} copy(bf16[2,8,12,1024]{3,2,1,0:T(8,128)(2,1)} %get-tuple-element.40) | data formatting | bytes 786432
  137.5 0.0 copy-start.8
  137.5 0.0 copy-start.9
  137.5 2.7 %copy.24 = bf16[2,16,24,1024]{3,2,1,0:T(8,128)(2,1)} copy(bf16[2,16,24,1024]{3,2,1,0:T(8,128)(2,1)} %get-tuple-element.49) | data formatting | bytes 3145728
  140.2 0.0 copy-done.8
  140.2 0.6 copy.25
  140.9 0.0 copy-done.9
  140.9 0.6 copy.26
Async XLA Ops:
  0.6 1.4 %copy-start.3 = (bf16[192,192]{1,0:T(8,128)(2,1)S(1)}, bf16[192,192]{1,0:T(8,128)(2,1)}, u32[]{:S(2)}) copy-start(bf16[192,192]{1,0:T(8,128)(2,1)} %constant.11.clone.merged_windows) | copy-start | bytes 221188
  0.6 1.4 %copy-start.4 = (bf16[192,192]{1,0:T(8,128)(2,1)S(1)}, bf16[192,192]{1,0:T(8,128)(2,1)}, u32[]{:S(2)}) copy-start(bf16[192,192]{1,0:T(8,128)(2,1)} %constant.10.clone.merged_natural) | copy-start | bytes 221188
  0.7 1.4 %copy-start.6 = (bf16[128,128]{1,0:T(8,128)(2,1)S(1)}, bf16[128,128]{1,0:T(8,128)(2,1)}, u32[]{:S(2)}) copy-start(bf16[128,128]{1,0:T(8,128)(2,1)} %constant.9.clone.to_quarters) | copy-start | bytes 98308
  0.7 1.4 %copy-start.7 = (bf16[128,128]{1,0:T(8,128)(2,1)S(1)}, bf16[128,128]{1,0:T(8,128)(2,1)}, u32[]{:S(2)}) copy-start(bf16[128,128]{1,0:T(8,128)(2,1)} %constant.8.clone.to_natural) | copy-start | bytes 98308
  28.5 1.3 copy-start
  29.8 1.2 copy-start.1
  31.0 1.1 copy-start.2
  32.1 0.7 copy-start.5
  137.5 2.7 %copy-start.8 = (f32[8,3072]{1,0:T(8,128)S(1)}, f32[8,3072]{1,0:T(8,128)}, u32[]{:S(2)}) copy-start(f32[8,3072]{1,0:T(8,128)} %get-tuple-element.50) | copy-start | bytes 294916
  137.5 3.4 %copy-start.9 = (f32[8,1024]{1,0:T(8,128)S(1)}, f32[8,1024]{1,0:T(8,128)}, u32[]{:S(2)}) copy-start(f32[8,1024]{1,0:T(8,128)} %get-tuple-element.51) | copy-start | bytes 98308

commit v5 on v4

--- a/solution.py
+++ b/solution.py
@@ -14,10 +14,6 @@
 MIB = 1024 * 1024
 NT = (((1,), (1,)), ((), ()))
 TN = (((0,), (0,)), ((), ()))
-
-
-def params(limit=60):
-    return pltpu.CompilerParams(vmem_limit_bytes=limit * MIB)
 
 
 def dot(left, right, dims=(((1,), (0,)), ((), ()))):
@@ -373,8 +369,23 @@
     )(q, k, v, mix, mix_grad, normed_turned, mix_turned, grad, x, qkv_weight, merged_groups, *orders())
 
 
-def enter_kernel(tokens, merged_grad, to_natural, to_quarters, merged_natural, merged_windows,
-                 x_out, normed_out, normed_turned, groups_out, units, merged_units, send, recv):
+def front_kernel(tokens, merged_grad, weight_hbm, out_weight_hbm, merge_weight_hbm,
+                 to_natural, to_quarters, merged_natural, merged_windows,
+                 x_hbm, normed_hbm, q_hbm, k_hbm, v_hbm, mix_hbm, mix_turned_hbm, grad_hbm, mix_grad_hbm, merged_out,
+                 x, normed, normed_turned, q, k, v, mix, mix_turned, grad, mix_grad,
+                 qkv_weight, out_weight, merge_weight, scaled, change, inverses, groups, units, merged_units,
+                 load, store, send, recv):
+    loads = [pltpu.make_async_copy(source, target, load.at[i]) for i, (source, target) in enumerate(
+        ((weight_hbm, qkv_weight), (out_weight_hbm, out_weight), (merge_weight_hbm, merge_weight)))]
+    for copy in loads:
+        copy.start()
+    stores = []
+
+    def keep(source, target):
+        copy = pltpu.make_async_copy(source, target, store.at[len(stores)])
+        copy.start()
+        stores.append(copy)
+
     before, after = neighbours(-1), neighbours(1)
     greet(before, after)
     copies = (frame_copies(units, (4, 6), (0, 0), send, recv, 0, after)
@@ -403,143 +414,157 @@
         quarters = [units[2 * wa + u, 2 * wb + side] for u in range(2) for side in range(2)]
         values = dot(to_quarters[...], jnp.concatenate(quarters, axis=0))
         rows = pl.ds(w * 128, 128)
-        x_out[rows] = values.astype(BF16)
-        centered, inverse = statistics(values)
-        normed = centered * inverse
-        normed_out[rows] = normed.astype(BF16)
-        normed_turned[:, rows] = normed.T.astype(BF16)
+        x[rows] = values.astype(BF16)
+        for i in range(4):
+            centered, inverse = statistics(values[32 * i:32 * i + 32])
+            normed[pl.ds(w * 128 + 32 * i, 32)] = (centered * inverse).astype(BF16)
+        normed_turned[:, rows] = normed[rows].T
+
+    lane = lax.broadcasted_iota(jnp.int32, (128, 128), 1)
+    masks = [lane // 32 == head for head in range(4)]
+    edge = lax.axis_index("lat") == 0
+
+    def attend(half):
+        tokens_here = pl.ds(half * 384, 384)
+
+        def columns_of(chunk):
+            low = pl.multiple_of(chunk * 256, 256)
+            for third, target in enumerate((q, k, v)):
+                weight = qkv_weight[:, pl.ds(pl.multiple_of(third * 1024 + chunk * 256, 256), 256)]
+                target[tokens_here, pl.ds(low, 256)] = dot(normed[tokens_here], weight).astype(BF16)
+            for w in range(3):
+                rows = pl.ds(half * 384 + w * 128, 128)
+                for group in range(2):
+                    lanes = pl.ds(pl.multiple_of(low + group * 128, 128), 128)
+                    scores = dot(q[rows, lanes], stack(k[rows, lanes], masks), NT)
+                    weights = jnp.exp(scores * SCALE)
+                    if half == 0:
+                        weights = jnp.where(other_region(128, 512, edge), 0.0, weights)
+                    pieces = []
+                    for head in range(4):
+                        piece = weights[:, head * 128:head * 128 + 128]
+                        pieces.append((piece * (1.0 / jnp.sum(piece, axis=-1, keepdims=True))).astype(BF16))
+                    mixture = select(dot(jnp.concatenate(pieces, axis=0), v[rows, lanes]), masks)
+                    mix[rows, lanes] = mixture.astype(BF16)
+                    mix_turned[lanes, rows] = mixture.T.astype(BF16)
+
+        pl.loop(0, 4)(columns_of)
 
     window(4)
     window(5)
     copies[1].wait_recv()
     window(3)
-    for copy in copies[3:]:
-        copy.wait_recv()
-    groups = jnp.concatenate([merged_units[i, 0:6].reshape(48, 1024) for i in range(4)], axis=0)
-    groups_out[...] = dot(merged_windows[...], groups.astype(BF16)).astype(BF16)
+    loads[0].wait()
+    attend(1)
     copies[0].wait_recv()
     window(1)
     window(2)
     copies[2].wait_recv()
     window(0)
+    keep(x, x_hbm)
+    keep(normed_turned, normed_hbm)
+    attend(0)
+    for source, target in ((q, q_hbm), (k, k_hbm), (v, v_hbm), (mix, mix_hbm), (mix_turned, mix_turned_hbm)):
+        keep(source, target)
+    for copy in copies[3:]:
+        copy.wait_recv()
+    framed = jnp.concatenate([merged_units[i, 0:6].reshape(48, 1024) for i in range(4)], axis=0)
+    groups[...] = dot(merged_windows[...], framed.astype(BF16)).astype(BF16)
+    loads[1].wait()
+
+    def add_branch(chunk):
+        columns = pl.ds(pl.multiple_of(chunk * 256, 256), 256)
+        scaled[:, columns] = x[:, columns].astype(F32) + dot(mix[...], out_weight[:, columns])
+
+    pl.loop(0, 4)(add_branch)
+
+    def quarter_rows(i):
+        return [pl.ds(pl.multiple_of(i // 2 * 128 + j * 32 + i % 2 * 16, 16), 16) for j in range(4)]
+
+    def group_rows(i):
+        return [pl.ds(pl.multiple_of(j * 192 + i * 16, 16), 16) for j in range(4)]
+
+    def normalize_groups(i):
+        parts = [scaled[rows].astype(BF16).astype(F32) for rows in quarter_rows(i)]
+        center = sum(jnp.sum(part, axis=-1, keepdims=True) for part in parts) * (1 / 4096)
+        parts = [part - center for part in parts]
+        spread = sum(jnp.sum(jnp.square(part), axis=-1, keepdims=True) for part in parts) * (1 / 4096)
+        inverse = lax.rsqrt(spread + epsilon)
+        inverses[pl.ds(pl.multiple_of(i * 16, 16), 16)] = jnp.broadcast_to(inverse, (16, 128))
+        for part, rows in zip(parts, group_rows(i)):
+            normed[rows] = (part * inverse).astype(BF16)
+        for part, rows in zip(parts, quarter_rows(i)):
+            scaled[rows] = part * inverse
+
+    pl.loop(0, 12)(normalize_groups)
+    loads[2].wait()
+
+    def merge_columns(chunk):
+        columns = pl.ds(pl.multiple_of(chunk * 256, 256), 256)
+        total = dot(normed[0:192], merge_weight[0:1024, columns])
+        for j in range(1, 4):
+            total = total + dot(normed[192 * j:192 * j + 192], merge_weight[1024 * j:1024 * j + 1024, columns])
+        merged_out[:, columns] = total.astype(BF16)
+        for j in range(4):
+            rows = pl.ds(pl.multiple_of(j * 1024 + chunk * 256, 256), 256)
+            change[192 * j:192 * j + 192, columns] = dot(groups[...], merge_weight[rows], NT)
+
+    pl.loop(0, 4)(merge_columns)
+
+    def group_grads(i):
+        changes = [change[rows].astype(BF16).astype(F32) for rows in group_rows(i)]
+        values = [scaled[rows] for rows in quarter_rows(i)]
+        first = sum(jnp.sum(part, axis=-1, keepdims=True) for part in changes) * (1 / 4096)
+        second = sum(jnp.sum(part * value, axis=-1, keepdims=True) for part, value in zip(changes, values)) * (1 / 4096)
+        inverse = inverses[pl.ds(pl.multiple_of(i * 16, 16), 16), 0:1]
+        for part, value, rows in zip(changes, values, quarter_rows(i)):
+            grad[rows] = (inverse * (part - first - value * second)).astype(BF16)
+
+    pl.loop(0, 12)(group_grads)
+    keep(grad, grad_hbm)
+
+    def mixture_grads(chunk):
+        rows = pl.ds(pl.multiple_of(chunk * 256, 256), 256)
+        mix_grad[:, rows] = dot(grad[...], out_weight[rows], NT).astype(BF16)
+
+    pl.loop(0, 4)(mixture_grads)
+    keep(mix_grad, mix_grad_hbm)
+    for copy in stores:
+        copy.wait()
     for copy in copies:
         copy.wait_send()
 
 
-def enter(tokens, merged_grad):
-    vmem = pl.BlockSpec(memory_space=pltpu.VMEM)
-    grid_tokens = jax.ShapeDtypeStruct((768, 1024), BF16)
+def front(tokens, merged_grad, qkv_weight, out_weight, merge_weight):
+    vmem, anywhere = pl.BlockSpec(memory_space=pltpu.VMEM), pl.BlockSpec(memory_space=pl.ANY)
+    rows, turned = jax.ShapeDtypeStruct((768, 1024), BF16), jax.ShapeDtypeStruct((1024, 768), BF16)
+    rows_vmem, turned_vmem = pltpu.VMEM((768, 1024), BF16), pltpu.VMEM((1024, 768), BF16)
     return pl.pallas_call(
-        enter_kernel,
-        out_shape=(grid_tokens, grid_tokens, jax.ShapeDtypeStruct((1024, 768), BF16),
-                   jax.ShapeDtypeStruct((192, 1024), BF16)),
-        in_specs=[vmem] * 6,
-        out_specs=(vmem,) * 4,
+        front_kernel,
+        out_shape=(rows, turned, rows, rows, rows, rows, turned, rows, rows, jax.ShapeDtypeStruct((192, 1024), BF16)),
+        in_specs=[vmem] * 2 + [anywhere] * 3 + [vmem] * 4,
+        out_specs=(anywhere,) * 9 + (vmem,),
         scratch_shapes=[
+            rows_vmem, rows_vmem, turned_vmem, rows_vmem, rows_vmem, rows_vmem, rows_vmem, turned_vmem, rows_vmem,
+            rows_vmem,
+            pltpu.VMEM((1024, 3072), BF16), pltpu.VMEM((1024, 1024), BF16), pltpu.VMEM((4096, 1024), BF16),
+            pltpu.VMEM((768, 1024), F32), pltpu.VMEM((768, 1024), F32), pltpu.VMEM((192, 128), F32),
+            pltpu.VMEM((192, 1024), BF16),
             pltpu.VMEM((5, 7, 32, 1024), BF16),
             pltpu.VMEM((5, 7, 8, 1024), F32),
+            pltpu.SemaphoreType.DMA((3,)),
+            pltpu.SemaphoreType.DMA((9,)),
             pltpu.SemaphoreType.DMA((6,)),
             pltpu.SemaphoreType.DMA((6,)),
         ],
-        compiler_params=pltpu.CompilerParams(collective_id=1, has_side_effects=True, vmem_limit_bytes=48 * MIB),
-        name="enter",
-    )(tokens, merged_grad, *orders())
-
-
-def attend_kernel(normed, wq, wk, wv, q_out, k_out, v_out, mix_out, mix_turned):
-    for out, weight in ((q_out, wq), (k_out, wk), (v_out, wv)):
-        out[...] = dot(normed[...], weight[...]).astype(BF16)
-    lane = lax.broadcasted_iota(jnp.int32, (128, 128), 1)
-    masks = [lane // 32 == head for head in range(4)]
-    edge = lax.axis_index("lat") == 0
-    for w in range(6):
-        rows = pl.ds(w * 128, 128)
-        for group in range(2):
-            lanes = pl.ds(group * 128, 128)
-            scores = dot(q_out[rows, lanes], stack(k_out[rows, lanes], masks), NT)
-            weights = jnp.exp(scores * SCALE)
-            if w < 3:
-                weights = jnp.where(other_region(128, 512, edge), 0.0, weights)
-            pieces = []
-            for head in range(4):
-                piece = weights[:, head * 128:head * 128 + 128]
-                pieces.append((piece * (1.0 / jnp.sum(piece, axis=-1, keepdims=True))).astype(BF16))
-            mixture = select(dot(jnp.concatenate(pieces, axis=0), v_out[rows, lanes]), masks)
-            mix_out[rows, lanes] = mixture.astype(BF16)
-            mix_turned[lanes, rows] = mixture.T.astype(BF16)
-
-
-def attend(normed, qkv_weight):
-    tokens = jax.ShapeDtypeStruct((768, 1024), BF16)
-    block = pl.BlockSpec((768, 256), lambda c: (0, c))
-    weight = lambda third: pl.BlockSpec((1024, 256), lambda c: (0, third * 4 + c))
-    return pl.pallas_call(
-        attend_kernel,
-        grid=(4,),
-        out_shape=(tokens, tokens, tokens, tokens, jax.ShapeDtypeStruct((1024, 768), BF16)),
-        in_specs=[pl.BlockSpec((768, 1024), lambda c: (0, 0)), weight(0), weight(1), weight(2)],
-        out_specs=(block, block, block, block, pl.BlockSpec((256, 768), lambda c: (c, 0))),
-        compiler_params=params(), name="attend",
-    )(normed, qkv_weight, qkv_weight, qkv_weight)
-
-
-def merge_kernel(x, mixture, merged_grad, out_weight, merge_weight, merged_out, grad_out, mixture_grad,
-                 normed, total, normed_grad):
-    step = pl.program_id(0)
-
-    @pl.when(step == 0)
-    def _():
-        for w in range(6):
-            rows = pl.ds(w * 128, 128)
-            values = x[rows].astype(F32) + dot(mixture[rows], out_weight[...])
-            values = values.astype(BF16).astype(F32)
-            quarters = [values[32 * j:32 * j + 32] for j in range(4)]
-            center = sum(jnp.sum(part, axis=-1, keepdims=True) for part in quarters) * (1 / 4096)
-            quarters = [part - center for part in quarters]
-            spread = sum(jnp.sum(jnp.square(part), axis=-1, keepdims=True) for part in quarters) * (1 / 4096)
-            inverse = lax.rsqrt(spread + epsilon)
-            for j in range(4):
-                normed[j, pl.ds(w * 32, 32)] = quarters[j] * inverse
-            total[1, pl.ds(w * 32, 32)] = jnp.broadcast_to(inverse, (32, 1024))
-        total[0] = jnp.zeros((192, 1024), F32)
-
-    total[0] += dot(normed[step].astype(BF16), merge_weight[...])
-    normed_grad[step] = dot(merged_grad[...], merge_weight[...], NT).astype(BF16).astype(F32)
-
-    @pl.when(step == 3)
-    def _():
-        merged_out[...] = total[0].astype(BF16)
-        for w in range(6):
-            part = pl.ds(w * 32, 32)
-            first = sum(jnp.sum(normed_grad[j, part], axis=-1, keepdims=True) for j in range(4)) * (1 / 4096)
-            second = sum(jnp.sum(normed_grad[j, part] * normed[j, part], axis=-1, keepdims=True)
-                         for j in range(4)) * (1 / 4096)
-            inverse = total[1, part]
-            for j in range(4):
-                value = inverse * (normed_grad[j, part] - first - normed[j, part] * second)
-                grad_out[pl.ds(w * 128 + j * 32, 32)] = value.astype(BF16)
-        mixture_grad[...] = dot(grad_out[...], out_weight[...], NT).astype(BF16)
-
-
-def merge_both(x, mixture, merged_grad, out_weight, merge_weight):
-    whole = lambda rows: pl.BlockSpec((rows, 1024), lambda j: (0, 0))
-    tokens = jax.ShapeDtypeStruct((768, 1024), BF16)
-    return pl.pallas_call(
-        merge_kernel,
-        grid=(4,),
-        out_shape=(jax.ShapeDtypeStruct((192, 1024), BF16), tokens, tokens),
-        in_specs=[whole(768), whole(768), whole(192), whole(1024), pl.BlockSpec((1024, 1024), lambda j: (j, 0))],
-        out_specs=(whole(192), whole(768), whole(768)),
-        scratch_shapes=[pltpu.VMEM((4, 192, 1024), F32), pltpu.VMEM((2, 192, 1024), F32),
-                        pltpu.VMEM((4, 192, 1024), F32)],
-        compiler_params=params(), name="merge_both",
-    )(x, mixture, merged_grad, out_weight, merge_weight)
+        compiler_params=pltpu.CompilerParams(collective_id=1, has_side_effects=True, vmem_limit_bytes=62 * MIB),
+        name="front",
+    )(tokens, merged_grad, qkv_weight, out_weight, merge_weight, *orders())
 
 
 def shards(tokens, qkv_weight, out_weight, merge_weight, merged_grad):
-    x, normed, normed_turned, merged_grad_groups = enter(tokens, merged_grad.reshape(192, 1024))
-    q, k, v, mixture, mix_turned = attend(normed, qkv_weight)
-    merged_groups, grad, mixture_grad = merge_both(x, mixture, merged_grad_groups, out_weight, merge_weight)
+    x, normed_turned, q, k, v, mixture, mix_turned, grad, mixture_grad, merged_groups = front(
+        tokens, merged_grad.reshape(192, 1024), qkv_weight, out_weight, merge_weight)
     qkv_weight_grad, out_weight_grad, tokens_grad, merged = back(
         q, k, v, mixture, mixture_grad, normed_turned, mix_turned, grad, x, qkv_weight, merged_groups)
     return (merged, tokens_grad, qkv_weight_grad, out_weight_grad)

time: 142 us -> 135 us (0.951)
  local copies, waits for them, and re-layouts: 11.7 us -> 8.04 us
  Pallas kernels: 129 us -> 126 us
    pallas_call x3 -> x1, Pallas kernels: 61.9 us -> 46.3 us  [front(): pl.pallas_call(front_kernel, out_shape=(rows, turned, rows, rows, rows, r...]
    pallas_call x1, Pallas kernels: 67.1 us -> 79.3 us  [back(): pl.pallas_call(back_kernel, out_shape=(jax.ShapeDtypeStruct((8, 3072), F3...]
    unnamed x25 -> x9, local copies, waits for them, and re-layouts: 11.6 us -> 7.21 us
where the time goes in v5:
time: 135 us; the launch traced here: 134 us
  Pallas kernels  126 us (93%)
  local copies, waits for them, and re-layouts  8.04 us (6%)
    pallas_call x1, Pallas kernels, back(): pl.pallas_call(back_kernel, out_shape=(jax.ShapeDtypeStruct((8, 3072), F3...  79.3 us
    pallas_call x1, Pallas kernels, front(): pl.pallas_call(front_kernel, out_shape=(rows, turned, rows, rows, rows, r...  46.3 us
    unnamed x9, local copies, waits for them, and re-layouts  7.21 us

profile of v5, /device:TPU:1, one launch (start us, length us, event | category | flops | bytes accessed | tf_op | source)
XLA Modules:
  0.0 134.3 jit_solution(12729051420583264487)
XLA Ops:
  0.6 1.2 copy.19
  1.9 0.8 reshape.11.merged_grad
  2.7 46.3 %front.1 = (bf16[768,1024]{1,0:T(8,128)(2,1)}, bf16[1024,768]{1,0:T(8,128)(2,1)}, bf16[768,1024]{1,0:T(8,128)(2,1)}, bf16[768,1024]{1,0:T(8,128)(2,1)}, bf16[768...) custom-call(bf16[2,16,24,1024]{3,2,1,0:T(8,128)(2,1)} %tokens.1, ...), custom_call_target="tpu_custom_call" | custom-call | tf_op jit(solution)/shard_map/front/pallas_call | solution.py:542
  49.0 79.3 %back.1 = (f32[8,3072]{1,0:T(8,128)}, f32[8,1024]{1,0:T(8,128)}, bf16[2,16,24,1024]{3,2,1,0:T(8,128)(2,1)}, bf16[2,8,12,1024]{3,2,1,0:T(8,128)(2,1)}) custom-call(bf16[768,1024]{1,0:T(8,128)(2,1)} %get-tuple-element.18.q_hbm, bf16[768,1024]{1,0:T(8,128)(2,1)} %get-tuple-element.19.k_hbm, bf16[768,1024]{1,0:T(8,128)(2,1)} %get-tuple-element.20.v_hbm, ...), custom_call_target="tpu_custom_call" | custom-call | tf_op jit(solution)/shard_map/back/pallas_call | solution.py:341
  128.3 2.0 %copy.20 = bf16[2,8,12,1024]{3,1,2,0:T(8,128)(2,1)} copy(bf16[2,8,12,1024]{3,2,1,0:T(8,128)(2,1)} %get-tuple-element.36) | data formatting | bytes 786432
  130.3 0.0 copy-start
  130.3 0.0 copy-start.1
  130.3 2.7 %copy.24 = bf16[2,16,24,1024]{3,2,1,0:T(8,128)(2,1)} copy(bf16[2,16,24,1024]{3,2,1,0:T(8,128)(2,1)} %get-tuple-element.45) | data formatting | bytes 3145728
  133.0 0.0 copy-done
  133.0 0.6 copy.25
  133.7 0.0 copy-done.1
  133.7 0.6 copy.26
Async XLA Ops:
  130.3 2.7 %copy-start = (f32[8,3072]{1,0:T(8,128)S(1)}, f32[8,3072]{1,0:T(8,128)}, u32[]{:S(2)}) copy-start(f32[8,3072]{1,0:T(8,128)} %get-tuple-element.46) | copy-start | bytes 294916
  130.3 3.4 %copy-start.1 = (f32[8,1024]{1,0:T(8,128)S(1)}, f32[8,1024]{1,0:T(8,128)}, u32[]{:S(2)}) copy-start(f32[8,1024]{1,0:T(8,128)} %get-tuple-element.47) | copy-start | bytes 98308
